TPU v7x, 32 devices: a whole 2x2x4 slice. The times are simulated.
32 devices in a mesh: pos: 4 (over y, core), stream: 8 (over z, x).
Axes of the slice: x: 2, y: 2, z: 4, core: 2. Of those that a mesh axis runs over, the one named last changes fastest.
Arguments:
- tokens_in: bfloat16 [8, 2048, 8192], P('stream', 'pos'), may hold values from -6 to 6
- proj_in: bfloat16 [8, 2048, 256], P('stream', 'pos'), may hold values from -1.75 to 1.75
- step_raw: bfloat16 [8, 2048, 128], P('stream', 'pos')
- decay_log: float32 [128], replicated, may hold values from -0.7 to 0.7
- head_skip_weight: float32 [128], replicated, may hold values from 0.5 to 1.5
- row_counts: int32 [4, 8, 8], replicated, may hold values from 32 to 96, as said below
Outputs:
- layer_out: bfloat16 [8, 2048, 8192], P('stream', 'pos')
Inputs may be any that keep to these rules, and one draw needn't show every extreme that they name: For each p, every row and every column of row_counts[p] sums to 512; all rows and columns of row_counts[p] hold the same list of values in some order, and the list splits into pairs whose sum is twice the list's mean; each row_counts[p] holds the value 96.
All inputs are finite; a program needn't handle non-finite values.
Results may differ from a plain program's by a relative error of at most 0.0037.
Values may be sent and summed in bfloat16 or wider, within the bound.
A program may use at most 256 MiB of HBM per device.

v0:
```python
import math

import jax
import jax.numpy as jnp
from jax import lax
from jax.sharding import PartitionSpec as P

BLOCK = 512


def entering(array, axis, combine, identity):
    peers, here = (lax.axis_size(axis), lax.axis_index(axis))
    everything = jax.tree.map(lambda part: lax.all_gather(part, axis), array)
    start = jax.tree.map(
        lambda part, zero: jnp.broadcast_to(jnp.asarray(zero, part.dtype), part.shape),
        array,
        identity,
    )

    def step(k, before):
        reached = k < here
        new = combine(before, jax.tree.map(lambda part: part[k], everything))
        return jax.tree.map(lambda a, b: jnp.where(reached, a, b), new, before)

    return lax.fori_loop(0, peers, step, start)


def block_parts(tokens, input_projections, steps_raw, decay_rates):
    length = tokens.shape[0]
    head_count = tokens.shape[1]
    state_size = input_projections.shape[1] // 2
    inputs = input_projections[:, :state_size]
    readout = input_projections[:, state_size:]
    discretization_deltas = jax.nn.softplus(steps_raw.astype(jnp.float32))
    cumulated = jnp.cumsum(discretization_deltas * decay_rates[None, :], axis=0)
    scores = jnp.dot(readout, inputs.T, preferred_element_type=jnp.float32)
    causal = (
        jnp.arange(length, dtype=jnp.int32)[:, None] >= jnp.arange(length, dtype=jnp.int32)[None, :]
    )
    group_size = math.gcd(head_count, 16)

    def one_group(first_head):
        cum_group = lax.dynamic_slice_in_dim(cumulated, first_head, group_size, 1)
        step_group = lax.dynamic_slice_in_dim(discretization_deltas, first_head, group_size, 1)
        token_group = lax.dynamic_slice_in_dim(tokens, first_head, group_size, 1)
        log_decay = jnp.where(
            causal[:, :, None], cum_group[:, None, :] - cum_group[None, :, :], -jnp.inf
        )
        weights = (scores[:, :, None] * jnp.exp(log_decay) * step_group[None, :, :]).astype(
            jnp.bfloat16
        )
        return jnp.einsum("tsh,shp->thp", weights, token_group, preferred_element_type=jnp.float32)

    first_heads = jnp.arange(head_count // group_size, dtype=jnp.int32) * group_size
    local_part = lax.map(one_group, first_heads)
    local_part = jnp.moveaxis(local_part, 0, 1).reshape(length, head_count, tokens.shape[2])
    ending = cumulated[-1]
    scaled = (
        (jnp.exp(ending[None, :] - cumulated) * discretization_deltas)[:, :, None] * tokens
    ).astype(jnp.bfloat16)
    carried = jnp.einsum("sn,shp->hnp", inputs, scaled, preferred_element_type=jnp.float32)
    return (local_part, cumulated, carried, jnp.exp(ending))


def block_output(local_part, cumulated, readout, tokens, head_skip_weight, carry_state):
    readable = carry_state.astype(jnp.bfloat16)
    inherited = jnp.einsum("tn,hnp->thp", readout, readable, preferred_element_type=jnp.float32)
    total = (
        local_part
        + jnp.exp(cumulated)[:, :, None] * inherited
        + head_skip_weight[None, :, None] * tokens.astype(jnp.float32)
    )
    return total.astype(jnp.bfloat16)


def combine_states(earlier, later):
    return (earlier[0] * later[0], later[0][:, None, None] * earlier[1] + later[1])


def on_device(tokens_in, proj_in, step_raw, decay_log, head_skip_weight, row_counts):
    stream_count = lax.axis_size("stream")
    stream_index = lax.axis_index("stream")
    place_index = lax.axis_index("pos")
    tokens = tokens_in[0]
    input_projections = proj_in[0]
    steps_raw = step_raw[0]
    local_rows = tokens.shape[0]
    inner_width = tokens.shape[1]
    head_count = steps_raw.shape[1]
    head_size = inner_width // head_count
    state_size = input_projections.shape[1] // 2
    capacity = 3 * local_rows // (2 * stream_count)
    decay_rates = -jnp.exp(decay_log)
    place_counts = lax.dynamic_index_in_dim(row_counts, place_index, 0, keepdims=False)
    send_counts = lax.dynamic_index_in_dim(place_counts, stream_index, 0, keepdims=False)
    recv_counts = lax.dynamic_index_in_dim(place_counts, stream_index, 1, keepdims=False)
    send_start = jnp.cumsum(send_counts) - send_counts
    slot_range = jnp.arange(capacity, dtype=jnp.int32)
    pick_rows = jnp.clip(send_start[:, None] + slot_range[None, :], 0, local_rows - 1).reshape(-1)
    send_tokens = jnp.take(tokens, pick_rows, axis=0).reshape(stream_count, capacity, inner_width)
    send_proj = jnp.take(input_projections, pick_rows, axis=0).reshape(
        stream_count, capacity, 2 * state_size
    )
    send_steps = jnp.take(steps_raw, pick_rows, axis=0).reshape(stream_count, capacity, head_count)
    arrived = (
        lax.all_to_all(send_tokens, "stream", split_axis=0, concat_axis=0, tiled=True),
        lax.all_to_all(send_proj, "stream", split_axis=0, concat_axis=0, tiled=True),
        lax.all_to_all(send_steps, "stream", split_axis=0, concat_axis=0, tiled=True),
    )
    recv_end = jnp.cumsum(recv_counts)
    recv_start = recv_end - recv_counts
    positions = jnp.arange(local_rows, dtype=jnp.int32)
    source = jnp.sum((recv_end[:, None] <= positions[None, :]).astype(jnp.int32), axis=0)
    chosen = (source[None, :] == jnp.arange(stream_count, dtype=jnp.int32)[:, None]).astype(
        jnp.int32
    )
    source_start = jnp.sum(chosen * recv_start[:, None], axis=0)
    flat_rows = source * capacity + positions - source_start
    ordered_tokens = jnp.take(
        arrived[0].reshape(stream_count * capacity, inner_width), flat_rows, axis=0
    )
    ordered_proj = jnp.take(
        arrived[1].reshape(stream_count * capacity, 2 * state_size), flat_rows, axis=0
    )
    ordered_steps = jnp.take(
        arrived[2].reshape(stream_count * capacity, head_count), flat_rows, axis=0
    )
    token_heads = ordered_tokens.reshape(local_rows, head_count, head_size)
    accumulated_attenuation = jnp.ones((head_count,), jnp.float32)
    total_state = jnp.zeros((head_count, state_size, head_size), jnp.float32)
    part_data = block_parts(token_heads, ordered_proj, ordered_steps, decay_rates)
    total_state = part_data[3][:, None, None] * total_state + part_data[2]
    accumulated_attenuation = accumulated_attenuation * part_data[3]
    incoming = entering(
        (accumulated_attenuation, total_state),
        "pos",
        combine_states,
        (jnp.ones_like(accumulated_attenuation), jnp.zeros_like(total_state)),
    )
    carry_state = incoming[1]
    pieces = block_output(
        part_data[0],
        part_data[1],
        ordered_proj[0:BLOCK, state_size:],
        token_heads,
        head_skip_weight,
        carry_state,
    )
    result = pieces.reshape(local_rows, inner_width)
    return result[None]


def solution(mesh):
    in_specs = (
        P("stream", "pos", None),
        P("stream", "pos", None),
        P("stream", "pos", None),
        P(),
        P(),
        P(),
    )
    out_specs = P("stream", "pos", None)
    return jax.shard_map(
        on_device, mesh=mesh, in_specs=in_specs, out_specs=out_specs, check_vma=False
    )
```

profile of v0, /device:TPU:0, one launch (start us, length us, event | category | flops | bytes accessed | tf_op | source)
XLA Modules:
  0.0 650.8 jit_solution(10245028167206563402)
XLA Ops:
  11.8 7.3 %all-to-all-start.2 = ((bf16[8,96,128]{2,1,0:T(8,128)(2,1)}), bf16[8,96,128]{2,1,0:T(8,128)(2,1)S(1)}, u32[]{:S(2)}, u32[]{:S(2)}) async-start(bf16[8,96,128]{2,1,0:T(8,128)(2,1)} %broadcast_select_fusion.3), calls=%async_computation.2 | async-start | bytes 393216 | tf_op jit(solution)/shard_map/all_to_all | solution.py:108
  21.7 26.4 %gather_fusion = bf16[768,8192]{1,0:T(8,128)(2,1)} fusion(bf16[512,8192]{1,0:T(8,128)(2,1)} %bitcast.98, s32[1024]{0:T(1024)S(1)} %pad_clamp_fusion.1), kind=kCustom, calls=%fused_computation | custom fusion | bytes 25168896 | tf_op jit(solution)/shard_map/jit(_take)/gather | solution.py:100
  49.1 6.0 all-to-all-start.1
  55.1 10.8 %broadcast_select_fusion = bf16[8,96,8192]{2,1,0:T(8,128)(2,1)} fusion(bf16[8,96,8192]{2,1,0:T(8,128)(2,1)} %bitcast.99, pred[8,96]{1,0:T(8,128)(4,1)S(1)} %compare_and_fusion), kind=kLoop, calls=%fused_computation.27 | loop fusion | flops 6291456 | bytes 25166592 | tf_op jit(solution)/shard_map/jit(_take)/select_n | solution.py:100
  78.0 266.0 %all-to-all-done = bf16[8,96,8192]{2,1,0:T(8,128)(2,1)} async-done(((bf16[8,96,8192]{2,1,0:T(8,128)(2,1)}), bf16[8,96,8192]{2,1,0:T(8,128)(2,1)}, u32[]{:S(2)}, u32[]{:S(2)}) %all-to-all-start) | async-done | bytes 12582944 | tf_op jit(solution)/shard_map/all_to_all | solution.py:106
  344.0 21.7 %gather_fusion.1 = bf16[512,8192]{1,0:T(8,128)(2,1)} fusion(bf16[768,8192]{1,0:T(8,128)(2,1)} %bitcast.6, s32[1024]{0:T(1024)S(1)} %pad_clamp_fusion), kind=kCustom, calls=%fused_computation.1 | custom fusion | bytes 16779264 | tf_op jit(solution)/shard_map/jit(_take)/gather | solution.py:119
  365.7 12.3 %copy.44 = bf16[512,8192]{0,1:T(8,128)(2,1)} copy(bf16[512,8192]{1,0:T(8,128)(2,1)} %gather_fusion.1) | data formatting | bytes 16777216 | tf_op jit(solution)/shard_map/jit(_take)/gather | solution.py:119
  378.0 16.5 %copy_select_fusion = bf16[512,128,64]{0,1,2:T(8,128)(2,1)} fusion(bf16[512,128,64]{0,2,1:T(8,128)(2,1)} %bitcast.100, pred[512]{0:T(512)(128)(4,1)S(1)} %compare_and_fusion.1), kind=kLoop, calls=%fused_computation.29 | loop fusion | flops 4194304 | bytes 16777728 | tf_op jit(solution)/shard_map/jit(_take)/select_n | solution.py:119
  394.5 7.9 %add_bitcast_fusion = f32[128,128,64]{1,0,2:T(8,128)} fusion(f32[128]{0:T(128)S(1)} %exponential_multiply_fusion.1, bf16[512,128,64]{0,1,2:T(8,128)(2,1)} %copy_select_fusion, f32[512,128]{0,1:T(8,128)S(1)} %copy.53, bf16[512,256]{1,0:T(8,128)(2,1)S(1)} %broadcast_select_fusion.2), kind=kOutput, calls=%fused_computation.31 | convolution fusion | flops 1087373312 | bytes 12976640 | tf_op jit(solution)/shard_map/sn,shp->hnp/dot_general | solution.py:61
  408.2 87.5 %while.25 = (s32[]{:T(128)}, f32[8,512,16,64]{1,3,2,0:T(8,128)}, s32[8]{0:T(128)S(1)}, bf16[512,128,64]{0,1,2:T(8,128)(2,1)}, f32[512,512]{1,0:T(8,128)S(1)}, /*...) while((s32[]{:T(128)}, f32[8,512,16,64]{1,3,2,0:T(8,128)}, ...), condition=%wide.region_7.8_spmd.clone, body=%wide.region_6.7_spmd.clone.sunk | while | flops 558104576 | bytes 7045287 | solution.py:55
  412.7 6.7 %bitcast_dynamic-update-slice_fusion.2 = f32[8,512,16,64]{1,3,2,0:T(8,128)} fusion(f32[8,512,16,64]{1,3,2,0:T(8,128)} %get-tuple-element.345, s32[]{:T(128)S(6)} %copy.72, f32[512,16]{0,1:T(8,128)S(1)} %get-tuple-element.327, f32[512,16]{0,1:T(8,128)S(1)} %get-tuple-element.328, f32[512,512]{1,0:T(8,128)S(1)} %get-tuple-element.358, ...), kind=kOutput, calls=%fused_computation.10.clone.1 | convolution fusion | flops 557842432 | bytes 4554756 | tf_op jit(solution)/shard_map/while/body/eval_jaxpr/tsh,shp->thp/dot_general | solution.py:52
  423.7 6.7 %bitcast_dynamic-update-slice_fusion.2 = f32[8,512,16,64]{1,3,2,0:T(8,128)} fusion(f32[8,512,16,64]{1,3,2,0:T(8,128)} %get-tuple-element.345, s32[]{:T(128)S(6)} %copy.72, f32[512,16]{0,1:T(8,128)S(1)} %get-tuple-element.327, f32[512,16]{0,1:T(8,128)S(1)} %get-tuple-element.328, f32[512,512]{1,0:T(8,128)S(1)} %get-tuple-element.358, ...), kind=kOutput, calls=%fused_computation.10.clone.1 | convolution fusion | flops 557842432 | bytes 4554756 | tf_op jit(solution)/shard_map/while/body/eval_jaxpr/tsh,shp->thp/dot_general | solution.py:52
  434.6 6.6 %bitcast_dynamic-update-slice_fusion.2 = f32[8,512,16,64]{1,3,2,0:T(8,128)} fusion(f32[8,512,16,64]{1,3,2,0:T(8,128)} %get-tuple-element.345, s32[]{:T(128)S(6)} %copy.72, f32[512,16]{0,1:T(8,128)S(1)} %get-tuple-element.327, f32[512,16]{0,1:T(8,128)S(1)} %get-tuple-element.328, f32[512,512]{1,0:T(8,128)S(1)} %get-tuple-element.358, ...), kind=kOutput, calls=%fused_computation.10.clone.1 | convolution fusion | flops 557842432 | bytes 4554756 | tf_op jit(solution)/shard_map/while/body/eval_jaxpr/tsh,shp->thp/dot_general | solution.py:52
  445.5 6.6 %bitcast_dynamic-update-slice_fusion.2 = f32[8,512,16,64]{1,3,2,0:T(8,128)} fusion(f32[8,512,16,64]{1,3,2,0:T(8,128)} %get-tuple-element.345, s32[]{:T(128)S(6)} %copy.72, f32[512,16]{0,1:T(8,128)S(1)} %get-tuple-element.327, f32[512,16]{0,1:T(8,128)S(1)} %get-tuple-element.328, f32[512,512]{1,0:T(8,128)S(1)} %get-tuple-element.358, ...), kind=kOutput, calls=%fused_computation.10.clone.1 | convolution fusion | flops 557842432 | bytes 4554756 | tf_op jit(solution)/shard_map/while/body/eval_jaxpr/tsh,shp->thp/dot_general | solution.py:52
  456.4 6.7 %bitcast_dynamic-update-slice_fusion.2 = f32[8,512,16,64]{1,3,2,0:T(8,128)} fusion(f32[8,512,16,64]{1,3,2,0:T(8,128)} %get-tuple-element.345, s32[]{:T(128)S(6)} %copy.72, f32[512,16]{0,1:T(8,128)S(1)} %get-tuple-element.327, f32[512,16]{0,1:T(8,128)S(1)} %get-tuple-element.328, f32[512,512]{1,0:T(8,128)S(1)} %get-tuple-element.358, ...), kind=kOutput, calls=%fused_computation.10.clone.1 | convolution fusion | flops 557842432 | bytes 4554756 | tf_op jit(solution)/shard_map/while/body/eval_jaxpr/tsh,shp->thp/dot_general | solution.py:52
  467.4 6.6 %bitcast_dynamic-update-slice_fusion.2 = f32[8,512,16,64]{1,3,2,0:T(8,128)} fusion(f32[8,512,16,64]{1,3,2,0:T(8,128)} %get-tuple-element.345, s32[]{:T(128)S(6)} %copy.72, f32[512,16]{0,1:T(8,128)S(1)} %get-tuple-element.327, f32[512,16]{0,1:T(8,128)S(1)} %get-tuple-element.328, f32[512,512]{1,0:T(8,128)S(1)} %get-tuple-element.358, ...), kind=kOutput, calls=%fused_computation.10.clone.1 | convolution fusion | flops 557842432 | bytes 4554756 | tf_op jit(solution)/shard_map/while/body/eval_jaxpr/tsh,shp->thp/dot_general | solution.py:52
  478.2 6.7 %bitcast_dynamic-update-slice_fusion.2 = f32[8,512,16,64]{1,3,2,0:T(8,128)} fusion(f32[8,512,16,64]{1,3,2,0:T(8,128)} %get-tuple-element.345, s32[]{:T(128)S(6)} %copy.72, f32[512,16]{0,1:T(8,128)S(1)} %get-tuple-element.327, f32[512,16]{0,1:T(8,128)S(1)} %get-tuple-element.328, f32[512,512]{1,0:T(8,128)S(1)} %get-tuple-element.358, ...), kind=kOutput, calls=%fused_computation.10.clone.1 | convolution fusion | flops 557842432 | bytes 4554756 | tf_op jit(solution)/shard_map/while/body/eval_jaxpr/tsh,shp->thp/dot_general | solution.py:52
  489.0 6.6 %bitcast_dynamic-update-slice_fusion.2 = f32[8,512,16,64]{1,3,2,0:T(8,128)} fusion(f32[8,512,16,64]{1,3,2,0:T(8,128)} %get-tuple-element.345, s32[]{:T(128)S(6)} %copy.72, f32[512,16]{0,1:T(8,128)S(1)} %get-tuple-element.327, f32[512,16]{0,1:T(8,128)S(1)} %get-tuple-element.328, f32[512,512]{1,0:T(8,128)S(1)} %get-tuple-element.358, ...), kind=kOutput, calls=%fused_computation.10.clone.1 | convolution fusion | flops 557842432 | bytes 4554756 | tf_op jit(solution)/shard_map/while/body/eval_jaxpr/tsh,shp->thp/dot_general | solution.py:52
  495.6 17.8 %copy.51 = f32[512,8,16,64]{0,2,1,3:T(8,128)} copy(f32[512,8,16,64]{0,3,2,1:T(8,128)} %bitcast.104) | data formatting | bytes 33554432 | tf_op jit(solution)/shard_map/transpose | solution.py:56
  513.4 82.2 %while.26 = (s32[]{:T(128)}, f32[128,128,64]{2,1,0:T(8,128)}, s32[]{:T(128)}, f32[4,128]{1,0:T(4,128)S(1)}, f32[4,128,128,64]{2,1,0,3:T(8,128)}, /*index=5*/s32[]{:T(128)}, s32[]{:T(128)}) while((s32[]{:T(128)}, f32[128,128,64]{2,1,0:T(8,128)}, s32[]{:T(128)}, f32[4,128]{1,0:T(4,128)S(1)}, f32[4,128,128,64]{2,1,0,3:T(8,128)}, ...), condition=%wide.region_9.10_spmd.clone, body=%wide.region_8.9_spmd.clone.sunk | while | flops 4194308 | bytes 29361776 | solution.py:25
  518.0 6.9 %copy.68 = f32[1,128,128,64]{3,2,1,0:T(8,128)} copy(f32[1,128,128,64]{2,1,0,3:T(8,128)} %constant_dynamic-slice_fusion.10) | data formatting | bytes 8388608 | tf_op jit(solution)/shard_map/while/body/eval_jaxpr/dynamic_slice | solution.py:22
  525.0 6.1 fusion.41
  535.6 6.9 %copy.68 = f32[1,128,128,64]{3,2,1,0:T(8,128)} copy(f32[1,128,128,64]{2,1,0,3:T(8,128)} %constant_dynamic-slice_fusion.10) | data formatting | bytes 8388608 | tf_op jit(solution)/shard_map/while/body/eval_jaxpr/dynamic_slice | solution.py:22
  542.6 10.0 %fusion.41 = f32[128,128,64]{2,1,0:T(8,128)} fusion(f32[1,128,128,64]{3,2,1,0:T(8,128)} %copy.68, f32[128,128,64]{2,1,0:T(8,128)} %get-tuple-element.372, f32[128]{0:T(128)S(1)} %dynamic-slice_bitcast_fusion.2, pred[]{:T(512)S(6)} %compare.3, pred[]{:T(512)S(6)} %lt.120), kind=kLoop, calls=%fused_computation.18.clone.1 | loop fusion | flops 4194304 | bytes 12583426 | tf_op jit(solution)/shard_map/while/body/eval_jaxpr/jit(_where)/select_n | solution.py:23
  557.2 6.9 %copy.68 = f32[1,128,128,64]{3,2,1,0:T(8,128)} copy(f32[1,128,128,64]{2,1,0,3:T(8,128)} %constant_dynamic-slice_fusion.10) | data formatting | bytes 8388608 | tf_op jit(solution)/shard_map/while/body/eval_jaxpr/dynamic_slice | solution.py:22
  564.1 10.0 %fusion.41 = f32[128,128,64]{2,1,0:T(8,128)} fusion(f32[1,128,128,64]{3,2,1,0:T(8,128)} %copy.68, f32[128,128,64]{2,1,0:T(8,128)} %get-tuple-element.372, f32[128]{0:T(128)S(1)} %dynamic-slice_bitcast_fusion.2, pred[]{:T(512)S(6)} %compare.3, pred[]{:T(512)S(6)} %lt.120), kind=kLoop, calls=%fused_computation.18.clone.1 | loop fusion | flops 4194304 | bytes 12583426 | tf_op jit(solution)/shard_map/while/body/eval_jaxpr/jit(_where)/select_n | solution.py:23
  578.7 6.9 %copy.68 = f32[1,128,128,64]{3,2,1,0:T(8,128)} copy(f32[1,128,128,64]{2,1,0,3:T(8,128)} %constant_dynamic-slice_fusion.10) | data formatting | bytes 8388608 | tf_op jit(solution)/shard_map/while/body/eval_jaxpr/dynamic_slice | solution.py:22
  585.6 10.0 %fusion.41 = f32[128,128,64]{2,1,0:T(8,128)} fusion(f32[1,128,128,64]{3,2,1,0:T(8,128)} %copy.68, f32[128,128,64]{2,1,0:T(8,128)} %get-tuple-element.372, f32[128]{0:T(128)S(1)} %dynamic-slice_bitcast_fusion.2, pred[]{:T(512)S(6)} %compare.3, pred[]{:T(512)S(6)} %lt.120), kind=kLoop, calls=%fused_computation.18.clone.1 | loop fusion | flops 4194304 | bytes 12583426 | tf_op jit(solution)/shard_map/while/body/eval_jaxpr/jit(_where)/select_n | solution.py:23
  595.6 6.3 convert_element_type.35
  606.7 13.7 %fusion.9 = bf16[512,128,64]{0,1,2:T(8,128)(2,1)} fusion(bf16[512,128,64]{0,1,2:T(8,128)(2,1)} %get-tuple-element.386, f32[512,8,16,64]{0,2,1,3:T(8,128)} %copy.51, bf16[128,128,64]{1,0,2:T(8,128)(2,1)S(1)} %copy.55, f32[128]{0:T(128)S(1)} %copy-done.2, f32[512,128]{0,1:T(8,128)S(1)} %copy.52, bf16[512,256]{1,0:T(8,128)(2,1)S(1)} %broadcast_select_fusion.2), kind=kOutput, calls=%fused_computation.25 | convolution fusion | flops 1098907648 | bytes 36045312 | tf_op jit(solution)/shard_map/tn,hnp->thp/dot_general | solution.py:67
  620.4 11.3 %copy.56 = bf16[512,128,64]{0,2,1:T(8,128)(2,1)} copy(bf16[512,128,64]{0,1,2:T(8,128)(2,1)} %fusion.9) | data formatting | bytes 16777216 | tf_op jit(solution)/shard_map/convert_element_type | solution.py:73
  631.8 12.0 %copy.57 = bf16[1,512,8192]{2,1,0:T(8,128)(2,1)} copy(bf16[1,512,8192]{1,2,0:T(8,128)(2,1)} %bitcast.101) | data formatting | bytes 16777216 | tf_op jit(solution)/shard_map/broadcast_in_dim;reshape | solution.py:150
  (100 shorter events, 70.4 us)
Async XLA Ops:
  6.5 12.5 %copy-start = (bf16[1,512,256]{2,1,0:T(8,128)(2,1)S(1)}, bf16[1,512,256]{2,1,0:T(8,128)(2,1)}, u32[]{:S(2)}) copy-start(bf16[1,512,256]{2,1,0:T(8,128)(2,1)} %param.11) | copy-start | bytes 786436
  11.8 37.3 %all-to-all-start.2 = ((bf16[8,96,128]{2,1,0:T(8,128)(2,1)}), bf16[8,96,128]{2,1,0:T(8,128)(2,1)S(1)}, u32[]{:S(2)}, u32[]{:S(2)}) async-start(bf16[8,96,128]{2,1,0:T(8,128)(2,1)} %broadcast_select_fusion.3), calls=%async_computation.2 | async-start | bytes 393216 | tf_op jit(solution)/shard_map/all_to_all | solution.py:108
  49.1 17.1 %all-to-all-start.1 = ((bf16[8,96,256]{2,1,0:T(8,128)(2,1)}), bf16[8,96,256]{2,1,0:T(8,128)(2,1)S(1)}, u32[]{:S(2)}, u32[]{:S(2)}) async-start(bf16[8,96,256]{2,1,0:T(8,128)(2,1)} %broadcast_select_fusion.1), calls=%async_computation.1 | async-start | bytes 786432 | tf_op jit(solution)/shard_map/all_to_all | solution.py:107
  65.9 7.6 %copy-start.3 = (f32[128]{0:T(128)S(1)}, f32[128]{0:T(128)}, u32[]{:S(2)}) copy-start(f32[128]{0:T(128)} %param.13) | copy-start | bytes 1540
  66.2 277.8 %all-to-all-start = ((bf16[8,96,8192]{2,1,0:T(8,128)(2,1)}), bf16[8,96,8192]{2,1,0:T(8,128)(2,1)}, u32[]{:S(2)}, u32[]{:S(2)}) async-start(bf16[8,96,8192]{2,1,0:T(8,128)(2,1)} %broadcast_select_fusion), calls=%async_computation | async-start | bytes 25165824 | tf_op jit(solution)/shard_map/all_to_all | solution.py:106
  72.0 441.4 %all-gather.4.cloned.1.call-start = ((), (), s32[]{:S(2)}) async-start(), calls=%async_computation.3 | async-start | bytes 20971520 | tf_op jit(solution)/shard_map/all_gather | solution.py:13
  595.6 11.1 %copy-start.2 = (f32[128]{0:T(128)S(1)}, f32[128]{0:T(128)}, u32[]{:S(2)}) copy-start(f32[128]{0:T(128)} %param.14) | copy-start | bytes 1540
  631.8 12.0 %copy-start.1 = (bf16[1,512,256]{2,1,0:T(8,128)(2,1)S(1)}, bf16[1,512,256]{2,1,0:T(8,128)(2,1)}, u32[]{:S(2)}) copy-start(bf16[1,512,256]{2,1,0:T(8,128)(2,1)} %param.11) | copy-start | bytes 786436
Sparse Core Ops, SparseCore 0:
  402.5 105.0 all-gather.3
where the time goes:
time: 661 us; the launch traced here: 651 us
  waiting for transfers between devices  266 us (40%)
  local copies, waits for them, and re-layouts  183 us (28%)
  matrix products  75 us (11%)
  other arithmetic  74.4 us (11%)
  starting transfers between devices  19.3 us (3%)
  between operations  13.9 us (2%)
  loops' own time  13.7 us (2%)
    all_to_all x1, waiting for transfers between devices, on_device(): lax.all_to_all(send_tokens, 'stream', split_axis=0, concat_axis=0, tiled=...  266 us
    dot_general x8, matrix products, one_group(): jnp.einsum('tsh,shp->thp', weights, token_group, preferred_element_type=j...  53.2 us
    dynamic_slice x8, local copies, waits for them, and re-layouts, step(): new = combine(before, jax.tree.map(lambda part: part[k], everything))  46.2 us
    select_n x4, other arithmetic, step(): return jax.tree.map(lambda a, b: jnp.where(reached, a, b), new, before)  36 us
    gather x2, local copies, waits for them, and re-layouts, on_device(): jnp.take(arrived[0].reshape(stream_count * capacity, inner_width), flat_r...  34 us
    gather x1, local copies, waits for them, and re-layouts, on_device(): jnp.take(tokens, pick_rows, axis=0)  26.4 us
    transpose x1, local copies, waits for them, and re-layouts, block_parts(): jnp.moveaxis(local_part, 0, 1).reshape(length, head_count, tokens.shape[2])  17.8 us
    select_n x1, other arithmetic, on_device(): jnp.take(arrived[0].reshape(stream_count * capacity, inner_width), flat_r...  16.5 us
  transfers between devices with their start and end apart: 4, of which 2 were waited for; matrix products, arithmetic and copies ran while one was open for 21% of the time, Pallas kernels for 0%

commit v1 on v0

v1 whole, which is shorter than its diff:
```python
import jax
import jax.numpy as jnp
from jax import lax
from jax.experimental import pallas as pl
from jax.experimental.pallas import tpu as pltpu
from jax.sharding import PartitionSpec as P

TILE_HEADS = 8
ROWS = 128
GROUPS = (4, 4, 4, 2, 2)
LOG2E = 1.4426950408889634
VMEM = 40 * 1024 * 1024


def expand(factors, pair, low):
    return jnp.where(low, factors[:, 2 * pair : 2 * pair + 1], factors[:, 2 * pair + 1 : 2 * pair + 2])


def state_kernel(order_ref, arrived_ref, inputs_t_ref, factor_ref, x_ref, carried_ref, scaled_ref):
    x = jnp.dot(order_ref[...], arrived_ref[...], preferred_element_type=jnp.float32)
    x_ref[...] = x.astype(jnp.bfloat16)
    factors = factor_ref[0]
    rows = x.shape[0]
    low = lax.broadcasted_iota(jnp.int32, (rows, 128), 1) < 64
    for pair in range(TILE_HEADS // 2):
        part = slice(128 * pair, 128 * pair + 128)
        scaled_ref[:, part] = (expand(factors, pair, low) * x[:, part]).astype(jnp.bfloat16)
    carried_ref[...] = jnp.dot(
        inputs_t_ref[...], scaled_ref[...], preferred_element_type=jnp.float32
    ).astype(jnp.bfloat16)


def output_kernel(
    x_ref,
    scores_ref,
    readout_ref,
    cum_ref,
    grow_ref,
    source_ref,
    carried_ref,
    coef_ref,
    skip_ref,
    *rest,
):
    out_ref, inherited_ref = rest[-2:]
    peers = carried_ref.shape[0]
    state = coef_ref[0:1, :] * carried_ref[0].astype(jnp.float32)
    for k in range(1, peers):
        state = state + coef_ref[k : k + 1, :] * carried_ref[k].astype(jnp.float32)
    inherited_ref[...] = jnp.dot(
        readout_ref[...], state.astype(jnp.bfloat16), preferred_element_type=jnp.float32
    )
    length = x_ref.shape[0]
    low = lax.broadcasted_iota(jnp.int32, (length, 128), 1) < 64
    low_rows = low[:ROWS]
    causal = lax.broadcasted_iota(jnp.int32, (ROWS, ROWS), 0) >= lax.broadcasted_iota(
        jnp.int32, (ROWS, ROWS), 1
    )
    cum = cum_ref[0]
    grow = grow_ref[0]
    source = source_ref[0]
    for pair in range(TILE_HEADS // 2):
        part = slice(128 * pair, 128 * pair + 128)
        x = x_ref[:, part]
        zero = jnp.zeros_like(x)
        halves = (jnp.where(low, x, zero), jnp.where(low, zero, x))
        for tile in range(length // ROWS):
            here = slice(ROWS * tile, ROWS * tile + ROWS)
            total = expand(grow[here], pair, low_rows) * inherited_ref[here, part]
            total = total + skip_ref[:, part] * x[here].astype(jnp.float32)
            for which in range(2):
                head = 2 * pair + which
                last = cum[here, head : head + 1]
                pieces = []
                if tile:
                    gap = last - source[head : head + 1, : ROWS * tile]
                    pieces.append(
                        (scores_ref[here, : ROWS * tile] * jnp.exp2(gap)).astype(jnp.bfloat16)
                    )
                gap = jnp.where(causal, last - source[head : head + 1, here], -jnp.inf)
                pieces.append((scores_ref[here, here] * jnp.exp2(gap)).astype(jnp.bfloat16))
                weights = pieces[0] if len(pieces) == 1 else jnp.concatenate(pieces, axis=1)
                total = total + jnp.dot(
                    weights,
                    halves[which][: ROWS * (tile + 1)],
                    preferred_element_type=jnp.float32,
                )
            out_ref[here, part] = total.astype(jnp.bfloat16)


def states(order, arrived, inputs_t, factors, first, tiles, tile_cols):
    rows, slots = order.shape
    state_size = inputs_t.shape[0]
    cols = tiles * tile_cols
    return pl.pallas_call(
        state_kernel,
        grid=(tiles,),
        in_specs=[
            pl.BlockSpec((rows, slots), lambda i: (0, 0)),
            pl.BlockSpec((slots, tile_cols), lambda i: (0, i)),
            pl.BlockSpec((state_size, rows), lambda i: (0, 0)),
            pl.BlockSpec((1, rows, TILE_HEADS), lambda i: (first + i, 0, 0)),
        ],
        out_specs=[
            pl.BlockSpec((rows, tile_cols), lambda i: (0, i)),
            pl.BlockSpec((state_size, tile_cols), lambda i: (0, i)),
        ],
        out_shape=[
            jax.ShapeDtypeStruct((rows, cols), jnp.bfloat16),
            jax.ShapeDtypeStruct((state_size, cols), jnp.bfloat16),
        ],
        scratch_shapes=[pltpu.VMEM((rows, tile_cols), jnp.bfloat16)],
        compiler_params=pltpu.CompilerParams(vmem_limit_bytes=VMEM),
        cost_estimate=pl.CostEstimate(
            flops=2 * rows * slots * cols + 2 * rows * state_size * cols,
            bytes_accessed=2 * (slots + rows + state_size) * cols,
            transcendentals=0,
        ),
    )(order, arrived, inputs_t, factors)


def outputs(previous, x, scores, readout, cum, grow, source, carried, coef, skip, first, tiles, tile_cols):
    rows = x.shape[0]
    state_size = readout.shape[1]
    peers = carried.shape[0]
    cols = tiles * tile_cols
    whole = coef.shape[1]
    in_specs = [
        pl.BlockSpec((rows, tile_cols), lambda i: (0, i)),
        pl.BlockSpec((rows, rows), lambda i: (0, 0)),
        pl.BlockSpec((rows, state_size), lambda i: (0, 0)),
        pl.BlockSpec((1, rows, TILE_HEADS), lambda i: (first + i, 0, 0)),
        pl.BlockSpec((1, rows, TILE_HEADS), lambda i: (first + i, 0, 0)),
        pl.BlockSpec((1, TILE_HEADS, rows), lambda i: (first + i, 0, 0)),
        pl.BlockSpec((peers, state_size, tile_cols), lambda i: (0, 0, i)),
        pl.BlockSpec((peers, tile_cols), lambda i: (0, first + i)),
        pl.BlockSpec((1, tile_cols), lambda i: (0, first + i)),
    ]
    operands = [x, scores, readout, cum, grow, source, carried, coef, skip]
    aliases = {}
    if previous is not None:
        in_specs.append(pl.BlockSpec(memory_space=pl.ANY))
        aliases = {len(operands): 0}
        operands.append(previous)
    return pl.pallas_call(
        output_kernel,
        grid=(tiles,),
        in_specs=in_specs,
        out_specs=pl.BlockSpec((rows, tile_cols), lambda i: (0, first + i)),
        out_shape=jax.ShapeDtypeStruct((rows, whole), jnp.bfloat16),
        scratch_shapes=[pltpu.VMEM((rows, tile_cols), jnp.float32)],
        input_output_aliases=aliases,
        compiler_params=pltpu.CompilerParams(vmem_limit_bytes=VMEM),
        cost_estimate=pl.CostEstimate(
            flops=2 * rows * (rows * 3 + state_size) * cols,
            bytes_accessed=2 * (2 * rows + peers * state_size) * cols,
            transcendentals=rows * rows * TILE_HEADS * tiles,
        ),
    )(*operands)


def on_device(tokens_in, proj_in, step_raw, decay_log, head_skip_weight, row_counts):
    streams = lax.axis_size("stream")
    stream = lax.axis_index("stream")
    place = lax.axis_index("pos")
    peers = lax.axis_size("pos")
    tokens = tokens_in[0]
    rows, inner = tokens.shape
    heads = step_raw.shape[2]
    head_size = inner // heads
    state_size = proj_in.shape[2] // 2
    capacity = 3 * rows // (2 * streams)
    slots = streams * capacity
    tile_cols = TILE_HEADS * head_size
    all_tiles = heads // TILE_HEADS

    counts = lax.dynamic_index_in_dim(row_counts, place, 0, keepdims=False)
    sent = lax.dynamic_index_in_dim(counts, stream, 0, keepdims=False)
    received = lax.dynamic_index_in_dim(counts, stream, 1, keepdims=False)
    send_start = jnp.cumsum(sent) - sent
    recv_start = jnp.cumsum(received) - received
    slot = jnp.arange(capacity, dtype=jnp.int32)
    picked = (send_start[:, None] + slot[None, :]).reshape(slots)
    position = jnp.arange(rows, dtype=jnp.int32)
    pack = (picked[:, None] == position[None, :]).astype(jnp.bfloat16)
    landed = jnp.where(
        slot[None, :] < received[:, None], recv_start[:, None] + slot[None, :], -1
    ).reshape(slots)
    order = (position[:, None] == landed[None, :]).astype(jnp.bfloat16)

    def exchange(block):
        packed = jnp.dot(pack, block, preferred_element_type=jnp.bfloat16)
        packed = packed.reshape(streams, capacity, block.shape[1])
        arrived = lax.all_to_all(packed, "stream", split_axis=0, concat_axis=0, tiled=True)
        return arrived.reshape(slots, block.shape[1])

    small = exchange(jnp.concatenate([proj_in[0], step_raw[0]], axis=1))
    bounds = []
    first = 0
    for share in GROUPS:
        tiles = share * all_tiles // 16
        bounds.append((first, tiles))
        first += tiles
    arrivals = [
        exchange(tokens[:, a * tile_cols : (a + n) * tile_cols]) for a, n in bounds
    ]

    small = jnp.dot(order, small, preferred_element_type=jnp.bfloat16)
    inputs = small[:, :state_size]
    readout = small[:, state_size : 2 * state_size]
    steps = jax.nn.softplus(small[:, 2 * state_size :].astype(jnp.float32))
    cumulated = jnp.cumsum(steps * -jnp.exp(decay_log)[None, :], axis=0)
    ending = cumulated[-1]
    scores = jnp.dot(readout, inputs.T, preferred_element_type=jnp.float32)
    inputs_t = inputs.T

    def by_tile(array):
        return jnp.moveaxis(array.reshape(rows, all_tiles, TILE_HEADS), 1, 0)

    factors = by_tile(jnp.exp(ending[None, :] - cumulated) * steps)
    grow = by_tile(jnp.exp(cumulated))
    cum = by_tile(cumulated * LOG2E)
    source = (cumulated * LOG2E - jnp.log2(steps)).T.reshape(all_tiles, TILE_HEADS, rows)

    endings = lax.all_gather(ending, "pos")
    places = jnp.arange(peers, dtype=jnp.int32)
    between = (places[None, :] > places[:, None]) & (places[None, :] < place)
    exponent = jnp.sum(jnp.where(between[:, :, None], endings[None], 0.0), axis=1)
    coef = jnp.where((places < place)[:, None], jnp.exp(exponent), 0.0)
    coef = jnp.repeat(coef, head_size, axis=1)
    skip = jnp.repeat(head_skip_weight, head_size)[None, :]

    result = None
    for (a, n), arrived in zip(bounds, arrivals):
        x, carried = states(order, arrived, inputs_t, factors, a, n, tile_cols)
        gathered = lax.all_gather(carried, "pos")
        result = outputs(
            result, x, scores, readout, cum, grow, source, gathered, coef, skip, a, n, tile_cols
        )
    return result[None]


def solution(mesh):
    in_specs = (
        P("stream", "pos", None),
        P("stream", "pos", None),
        P("stream", "pos", None),
        P(),
        P(),
        P(),
    )
    return jax.shard_map(
        on_device,
        mesh=mesh,
        in_specs=in_specs,
        out_specs=P("stream", "pos", None),
        check_vma=False,
    )
```

time: 661 us -> 425 us (0.64); the launches traced: 651 us -> 423 us
  local copies, waits for them, and re-layouts: 183 us -> 71.9 us
  other arithmetic: 74.4 us -> 3.01 us
  Pallas kernels: 0 us -> 53.4 us
  matrix products: 75 us -> 25.6 us
  waiting for transfers between devices: 266 us -> 223 us
  loops' own time: 13.7 us -> 0 us
  starting transfers between devices: 19.3 us -> 27.5 us
    gather x7 -> x0, local copies, waits for them, and re-layouts: 69 us -> none  [the longest x2 34 us: on_device(): jnp.take(arrived[0].reshape(stream_count * capacity, inner_width), flat_r...]
    dynamic_slice x33 -> x1, local copies, waits for them, and re-layouts: 67 us -> 0.88 us  [on_device(): received = lax.dynamic_index_in_dim(counts, stream, 1, keepdims=False)]
    select_n x11 -> x2, other arithmetic: 65.2 us -> 0.14 us  [the longest x1 0.07 us: on_device(): jnp.where(slot[None, :] < received[:, None], recv_start[:, None] + slot[N...]
    unnamed x11 -> x80, local copies, waits for them, and re-layouts: 0.28 us -> 59.5 us
    pallas_call x0 -> x10, Pallas kernels: none -> 53.4 us  [the longest x5 31.2 us: outputs(): pl.pallas_call(output_kernel, grid=(tiles,), in_specs=in_specs, out_specs...]
    dot_general x11 -> x8, matrix products: 75 us -> 25.6 us  [the longest x6 24.7 us: exchange(): packed = jnp.dot(pack, block, preferred_element_type=jnp.bfloat16)]
    all_to_all x3 -> x6, waiting for transfers between devices: 266 us -> 223 us  [exchange(): lax.all_to_all(packed, 'stream', split_axis=0, concat_axis=0, tiled=True)]
    transpose x1 -> x0, local copies, waits for them, and re-layouts: 17.8 us -> none  [block_parts(): jnp.moveaxis(local_part, 0, 1).reshape(length, head_count, tokens.shape[2])]
  transfers between devices with their start and end apart: 4 -> 11, of which waited for: 2 -> 6; matrix products, arithmetic and copies ran while one was open for 21% -> 9% of each run, Pallas kernels for 0% -> 12%
where the time goes in v1:
time: 425 us; the launch traced here: 423 us
  waiting for transfers between devices  223 us (52%)
  local copies, waits for them, and re-layouts  71.9 us (17%)
  Pallas kernels  53.4 us (13%)
  starting transfers between devices  27.5 us (6%)
  matrix products  25.6 us (6%)
  between operations  13.4 us (3%)
  blocking collectives  5.03 us (1%)
    all_to_all x6, waiting for transfers between devices, exchange(): lax.all_to_all(packed, 'stream', split_axis=0, concat_axis=0, tiled=True)  223 us
    unnamed x80, local copies, waits for them, and re-layouts  59.5 us
    pallas_call x5, Pallas kernels, outputs(): pl.pallas_call(output_kernel, grid=(tiles,), in_specs=in_specs, out_specs...  31.2 us
    all_to_all x6, starting transfers between devices, exchange(): lax.all_to_all(packed, 'stream', split_axis=0, concat_axis=0, tiled=True)  27.1 us
    dot_general x6, matrix products, exchange(): packed = jnp.dot(pack, block, preferred_element_type=jnp.bfloat16)  24.7 us
    pallas_call x5, Pallas kernels, states(): pl.pallas_call(state_kernel, grid=(tiles,), in_specs=[pl.BlockSpec((rows,...  22.2 us
    reshape x3, local copies, waits for them, and re-layouts, by_tile(): return jnp.moveaxis(array.reshape(rows, all_tiles, TILE_HEADS), 1, 0)  9.7 us
  transfers between devices with their start and end apart: 11, of which 6 were waited for; matrix products, arithmetic and copies ran while one was open for 9% of the time, Pallas kernels for 12%

profile of v1, /device:TPU:0, one launch (start us, length us, event | category | flops | bytes accessed | tf_op | source)
XLA Modules:
  0.0 422.8 jit_solution(8179217505305868799)
XLA Ops:
  8.3 2.5 fusion.7
  10.7 7.2 %all-to-all-start.1 = ((bf16[8,96,384]{2,1,0:T(8,128)(2,1)}), bf16[8,96,384]{2,1,0:T(8,128)(2,1)S(1)}, u32[]{:S(2)}, u32[]{:S(2)}) async-start(bf16[8,96,384]{2,1,0:T(8,128)(2,1)} %bitcast.9), calls=%async_computation.1 | async-start | bytes 1179648 | tf_op jit(solution)/shard_map/all_to_all | solution.py:194
  18.0 5.1 %fusion = bf16[768,2048]{1,0:T(8,128)(2,1)} fusion(bf16[512,8192]{1,0:T(8,128)(2,1)} %bitcast.117, s32[768]{0:T(1024)S(1)} %add.60), kind=kOutput, calls=%fused_computation | convolution fusion | flops 1611005952 | bytes 5245952 | tf_op jit(solution)/shard_map/dot_general | solution.py:192
  23.1 10.8 %all-to-all-done.1 = bf16[8,96,384]{2,1,0:T(8,128)(2,1)S(1)} async-done(((bf16[8,96,384]{2,1,0:T(8,128)(2,1)}), bf16[8,96,384]{2,1,0:T(8,128)(2,1)S(1)}, u32[]{:S(2)}, u32[]{:S(2)}) %all-to-all-start.1) | async-done | bytes 589856 | tf_op jit(solution)/shard_map/all_to_all | solution.py:194
  34.7 3.7 all-to-all-start.5
  38.3 5.1 %fusion.2 = bf16[768,2048]{1,0:T(8,128)(2,1)} fusion(bf16[512,8192]{1,0:T(8,128)(2,1)} %bitcast.118, s32[768]{0:T(1024)S(1)} %add.60), kind=kOutput, calls=%fused_computation.2 | convolution fusion | flops 1611005952 | bytes 5245952 | tf_op jit(solution)/shard_map/dot_general | solution.py:192
  43.4 65.8 %all-to-all-done.5 = bf16[8,96,2048]{2,1,0:T(8,128)(2,1)S(1)} async-done(((bf16[8,96,2048]{2,1,0:T(8,128)(2,1)}), bf16[8,96,2048]{2,1,0:T(8,128)(2,1)S(1)}, u32[]{:S(2)}, u32[]{:S(2)}) %all-to-all-start.5) | async-done | bytes 3145760 | tf_op jit(solution)/shard_map/all_to_all | solution.py:194
  110.9 4.5 %all-to-all-start.4 = ((bf16[8,96,2048]{2,1,0:T(8,128)(2,1)}), bf16[8,96,2048]{2,1,0:T(8,128)(2,1)}, u32[]{:S(2)}, u32[]{:S(2)}) async-start(bf16[8,96,2048]{2,1,0:T(8,128)(2,1)} %bitcast.103), calls=%async_computation.4 | async-start | bytes 6291456 | tf_op jit(solution)/shard_map/all_to_all | solution.py:194
  116.9 5.1 %fusion.4 = bf16[768,2048]{1,0:T(8,128)(2,1)} fusion(bf16[512,8192]{1,0:T(8,128)(2,1)} %bitcast.119, s32[768]{0:T(1024)S(1)} %add.60), kind=kOutput, calls=%fused_computation.4 | convolution fusion | flops 1611005952 | bytes 5245952 | tf_op jit(solution)/shard_map/dot_general | solution.py:192
  124.6 2.7 copy.28
  127.3 58.3 %all-to-all-done.4 = bf16[8,96,2048]{2,1,0:T(8,128)(2,1)} async-done(((bf16[8,96,2048]{2,1,0:T(8,128)(2,1)}), bf16[8,96,2048]{2,1,0:T(8,128)(2,1)}, u32[]{:S(2)}, u32[]{:S(2)}) %all-to-all-start.4) | async-done | bytes 3145760 | tf_op jit(solution)/shard_map/all_to_all | solution.py:194
  185.6 4.5 %all-to-all-start.3 = ((bf16[8,96,2048]{2,1,0:T(8,128)(2,1)}), bf16[8,96,2048]{2,1,0:T(8,128)(2,1)}, u32[]{:S(2)}, u32[]{:S(2)}) async-start(bf16[8,96,2048]{2,1,0:T(8,128)(2,1)} %bitcast.102), calls=%async_computation.3 | async-start | bytes 6291456 | tf_op jit(solution)/shard_map/all_to_all | solution.py:194
  194.2 4.8 %shard_map.68 = (bf16[512,2048]{1,0:T(8,128)(2,1)S(1)}, bf16[128,2048]{1,0:T(8,128)(2,1)}) custom-call(bf16[512,768]{1,0:T(8,128)(2,1)S(1)} %fusion.10.order_ref, bf16[768,2048]{1,0:T(8,128)(2,1)S(1)} %bitcast.94, bf16[128,512]{1,0:T(8,128)(2,1)S(1)} %get-tuple-element.28.inputs_t_ref, f32[16,512,8]{2,1,0:T(8,128)S(1)} %bitcast.79), custom_call_target="tpu_custom_call" | custom-call | flops 1879048192 | bytes 5767168 | tf_op jit(solution)/shard_map/pallas_call | solution.py:95
  202.7 6.0 %shard_map.67 = (bf16[512,2048]{1,0:T(8,128)(2,1)S(1)}, bf16[128,2048]{1,0:T(8,128)(2,1)}) custom-call(bf16[512,768]{1,0:T(8,128)(2,1)S(1)} %fusion.10.order_ref, bf16[768,2048]{1,0:T(8,128)(2,1)} %bitcast.33.arrived_ref, bf16[128,512]{1,0:T(8,128)(2,1)S(1)} %get-tuple-element.28.inputs_t_ref, f32[16,512,8]{2,1,0:T(8,128)S(1)} %bitcast.80), custom_call_target="tpu_custom_call" | custom-call | flops 1879048192 | bytes 5767168 | tf_op jit(solution)/shard_map/pallas_call | solution.py:95
  210.0 3.5 fusion.6
  213.4 46.8 %all-to-all-done.3 = bf16[8,96,2048]{2,1,0:T(8,128)(2,1)} async-done(((bf16[8,96,2048]{2,1,0:T(8,128)(2,1)}), bf16[8,96,2048]{2,1,0:T(8,128)(2,1)}, u32[]{:S(2)}, u32[]{:S(2)}) %all-to-all-start.3) | async-done | bytes 3145760 | tf_op jit(solution)/shard_map/all_to_all | solution.py:194
  260.2 3.6 all-to-all-start.2
  266.3 6.0 %shard_map.66 = (bf16[512,2048]{1,0:T(8,128)(2,1)S(1)}, bf16[128,2048]{1,0:T(8,128)(2,1)}) custom-call(bf16[512,768]{1,0:T(8,128)(2,1)S(1)} %fusion.10.order_ref, bf16[768,2048]{1,0:T(8,128)(2,1)} %bitcast.30.arrived_ref, bf16[128,512]{1,0:T(8,128)(2,1)S(1)} %get-tuple-element.28.inputs_t_ref, f32[16,512,8]{2,1,0:T(8,128)S(1)} %bitcast.81), custom_call_target="tpu_custom_call" | custom-call | flops 1879048192 | bytes 5767168 | tf_op jit(solution)/shard_map/pallas_call | solution.py:95
  273.6 3.4 fusion.8
  277.1 24.0 %all-to-all-done.2 = bf16[8,96,1024]{2,1,0:T(8,128)(2,1)S(1)} async-done(((bf16[8,96,1024]{2,1,0:T(8,128)(2,1)}), bf16[8,96,1024]{2,1,0:T(8,128)(2,1)S(1)}, u32[]{:S(2)}, u32[]{:S(2)}) %all-to-all-start.2) | async-done | bytes 1572896 | tf_op jit(solution)/shard_map/all_to_all | solution.py:194
  302.2 3.6 all-to-all-start
  309.5 2.8 shard_map.65
  313.6 3.5 copy.30
  317.1 3.6 copy.31
  320.6 5.0 %all-gather.5 = f32[4,1,128]{2,1,0:T(1,128)S(1)} all-gather(f32[1,1,128]{2,1,0:T(1,128)S(1)} %bitcast.115), channel_id=1, replica_groups=mesh['pos'=4,'stream'=8] {'pos'}, dimensions={0}, use_global_device_ids=true | all-gather | bytes 2560 | tf_op jit(solution)/shard_map/all_gather | solution.py:225
  325.8 17.3 %all-to-all-done = bf16[8,96,1024]{2,1,0:T(8,128)(2,1)S(1)} async-done(((bf16[8,96,1024]{2,1,0:T(8,128)(2,1)}), bf16[8,96,1024]{2,1,0:T(8,128)(2,1)S(1)}, u32[]{:S(2)}, u32[]{:S(2)}) %all-to-all-start) | async-done | bytes 1572896 | tf_op jit(solution)/shard_map/all_to_all | solution.py:194
  345.2 2.7 shard_map.64
  357.5 7.6 %shard_map.69.rest_0_ = bf16[512,8192]{1,0:T(8,128)(2,1)} custom-call(bf16[512,2048]{1,0:T(8,128)(2,1)S(1)} %copy-done.26, f32[512,512]{1,0:T(8,128)S(1)} %fusion.27.scores_ref, bf16[512,128]{1,0:T(8,128)(2,1)S(1)} %copy.32.readout_ref, f32[16,512,8]{2,1,0:T(8,128)S(1)} %bitcast.84, f32[16,512,8]{2,1,0:T(8,128)S(1)} %bitcast.89, ...), custom_call_target="tpu_custom_call" | custom-call | flops 3489660928 | bytes 6291456 | tf_op jit(solution)/shard_map/pallas_call | solution.py:145
  372.7 7.6 %shard_map.70.rest_0_ = bf16[512,8192]{1,0:T(8,128)(2,1)} custom-call(bf16[512,2048]{1,0:T(8,128)(2,1)S(1)} %copy-done.20, f32[512,512]{1,0:T(8,128)S(1)} %fusion.27.scores_ref, bf16[512,128]{1,0:T(8,128)(2,1)S(1)} %copy.32.readout_ref, f32[16,512,8]{2,1,0:T(8,128)S(1)} %bitcast.85, f32[16,512,8]{2,1,0:T(8,128)S(1)} %bitcast.90, ...), custom_call_target="tpu_custom_call", output_to_operand_aliasing={{}: (9, {})} | custom-call | flops 3489660928 | bytes 6291456 | tf_op jit(solution)/shard_map/pallas_call | solution.py:145
  387.9 7.6 %shard_map.71.rest_0_ = bf16[512,8192]{1,0:T(8,128)(2,1)} custom-call(bf16[512,2048]{1,0:T(8,128)(2,1)S(1)} %copy-done.23, f32[512,512]{1,0:T(8,128)S(1)} %fusion.27.scores_ref, bf16[512,128]{1,0:T(8,128)(2,1)S(1)} %copy.32.readout_ref, f32[16,512,8]{2,1,0:T(8,128)S(1)} %bitcast.86, f32[16,512,8]{2,1,0:T(8,128)S(1)} %bitcast.91, ...), custom_call_target="tpu_custom_call", output_to_operand_aliasing={{}: (9, {})} | custom-call | flops 3489660928 | bytes 6291456 | tf_op jit(solution)/shard_map/pallas_call | solution.py:145
  401.1 4.2 shard_map.72.rest_0_
  412.1 4.2 shard_map.73
  (128 shorter events, 66.6 us)
Async XLA Ops:
  10.7 23.1 %all-to-all-start.1 = ((bf16[8,96,384]{2,1,0:T(8,128)(2,1)}), bf16[8,96,384]{2,1,0:T(8,128)(2,1)S(1)}, u32[]{:S(2)}, u32[]{:S(2)}) async-start(bf16[8,96,384]{2,1,0:T(8,128)(2,1)} %bitcast.9), calls=%async_computation.1 | async-start | bytes 1179648 | tf_op jit(solution)/shard_map/all_to_all | solution.py:194
  34.7 74.5 %all-to-all-start.5 = ((bf16[8,96,2048]{2,1,0:T(8,128)(2,1)}), bf16[8,96,2048]{2,1,0:T(8,128)(2,1)S(1)}, u32[]{:S(2)}, u32[]{:S(2)}) async-start(bf16[8,96,2048]{2,1,0:T(8,128)(2,1)} %bitcast.104), calls=%async_computation.5 | async-start | bytes 6291456 | tf_op jit(solution)/shard_map/all_to_all | solution.py:194
  109.2 1.7 copy-start.15
  109.2 7.4 %copy-start.37 = (f32[128]{0:T(128)S(1)}, f32[128]{0:T(128)}, u32[]{:S(2)}) copy-start(f32[128]{0:T(128)} %param.9) | copy-start | bytes 1540
  110.9 74.6 %all-to-all-start.4 = ((bf16[8,96,2048]{2,1,0:T(8,128)(2,1)}), bf16[8,96,2048]{2,1,0:T(8,128)(2,1)}, u32[]{:S(2)}, u32[]{:S(2)}) async-start(bf16[8,96,2048]{2,1,0:T(8,128)(2,1)} %bitcast.103), calls=%async_computation.4 | async-start | bytes 6291456 | tf_op jit(solution)/shard_map/all_to_all | solution.py:194
  116.8 5.1 %copy-start.35 = (bf16[8,96,384]{2,1,0:T(8,128)(2,1)S(1)}, bf16[8,96,384]{2,1,0:T(8,128)(2,1)}, u32[]{:S(2)}) copy-start(bf16[8,96,384]{2,1,0:T(8,128)(2,1)} %copy-done.34) | copy-start | bytes 1769476
  185.6 74.6 %all-to-all-start.3 = ((bf16[8,96,2048]{2,1,0:T(8,128)(2,1)}), bf16[8,96,2048]{2,1,0:T(8,128)(2,1)}, u32[]{:S(2)}, u32[]{:S(2)}) async-start(bf16[8,96,2048]{2,1,0:T(8,128)(2,1)} %bitcast.102), calls=%async_computation.3 | async-start | bytes 6291456 | tf_op jit(solution)/shard_map/all_to_all | solution.py:194
  190.1 159.8 %all-gather.20.cloned.1.call-start = ((), (), s32[]{:S(2)}) async-start(), calls=%async_computation.10 | async-start | bytes 2621440 | tf_op jit(solution)/shard_map/all_gather | solution.py:236
  190.1 2.2 copy-start
  192.3 1.9 copy-start.16
  200.4 164.7 %all-gather.18.cloned.1.call-start = ((), (), s32[]{:S(2)}) async-start(), calls=%async_computation.9 | async-start | bytes 2621440 | tf_op jit(solution)/shard_map/all_gather | solution.py:236
  200.5 2.2 copy-start.1
  260.2 40.8 %all-to-all-start.2 = ((bf16[8,96,1024]{2,1,0:T(8,128)(2,1)}), bf16[8,96,1024]{2,1,0:T(8,128)(2,1)S(1)}, u32[]{:S(2)}, u32[]{:S(2)}) async-start(bf16[8,96,1024]{2,1,0:T(8,128)(2,1)} %bitcast.108), calls=%async_computation.2 | async-start | bytes 3145728 | tf_op jit(solution)/shard_map/all_to_all | solution.py:194
  263.9 116.5 %all-gather.16.cloned.1.call-start = ((), (), s32[]{:S(2)}) async-start(), calls=%async_computation.8 | async-start | bytes 2621440 | tf_op jit(solution)/shard_map/all_gather | solution.py:236
  264.1 2.2 copy-start.2
  302.2 40.8 %all-to-all-start = ((bf16[8,96,1024]{2,1,0:T(8,128)(2,1)}), bf16[8,96,1024]{2,1,0:T(8,128)(2,1)S(1)}, u32[]{:S(2)}, u32[]{:S(2)}) async-start(bf16[8,96,1024]{2,1,0:T(8,128)(2,1)} %bitcast.107), calls=%async_computation | async-start | bytes 3145728 | tf_op jit(solution)/shard_map/all_to_all | solution.py:194
  305.8 89.6 %all-gather.14.cloned.1.call-start = ((), (), s32[]{:S(2)}) async-start(), calls=%async_computation.7 | async-start | bytes 1310720 | tf_op jit(solution)/shard_map/all_gather | solution.py:236
  305.9 2.2 copy-start.3
  309.5 3.9 copy-start.36
  313.3 91.9 %all-gather.12.cloned.1.call-start = ((), (), s32[]{:S(2)}) async-start(), calls=%async_computation.6 | async-start | bytes 1310720 | tf_op jit(solution)/shard_map/all_gather | solution.py:236
  343.0 2.2 copy-start.4
  349.9 2.2 copy-start.5
  352.0 2.2 copy-start.10
  365.2 2.2 copy-start.6
  367.3 2.2 copy-start.11
  380.3 2.2 copy-start.7
  382.5 2.2 copy-start.12
  387.9 7.6 %copy-start.29 = (bf16[512,1024]{1,0:T(8,128)(2,1)S(1)}, bf16[512,1024]{1,0:T(8,128)(2,1)}, u32[]{:S(2)}) copy-start(bf16[512,1024]{1,0:T(8,128)(2,1)} %copy-done.28) | copy-start | bytes 3145732
  395.5 2.2 copy-start.8
  397.6 2.2 copy-start.13
  405.2 2.2 copy-start.9
  407.4 2.2 copy-start.14
  (17 other events, 22.9 us)
Sparse Core Ops, SparseCore 0:
  200.5 23.8 all-gather.19
  226.0 22.5 all-gather.17
  273.7 23.7 all-gather.15
  313.4 18.1 all-gather.13
  349.2 15.8 all-gather.11

commit v2 on v1

--- a/solution.py
+++ b/solution.py
@@ -7,7 +7,7 @@
 
 TILE_HEADS = 8
 ROWS = 128
-GROUPS = (4, 4, 4, 2, 2)
+GROUPS = (4, 9, 3)
 LOG2E = 1.4426950408889634
 VMEM = 40 * 1024 * 1024
 
@@ -194,18 +194,22 @@
         arrived = lax.all_to_all(packed, "stream", split_axis=0, concat_axis=0, tiled=True)
         return arrived.reshape(slots, block.shape[1])
 
-    small = exchange(jnp.concatenate([proj_in[0], step_raw[0]], axis=1))
     bounds = []
     first = 0
     for share in GROUPS:
         tiles = share * all_tiles // 16
         bounds.append((first, tiles))
         first += tiles
+
+    def columns(group):
+        a, n = bounds[group]
+        return tokens[:, a * tile_cols : (a + n) * tile_cols]
+
     arrivals = [
-        exchange(tokens[:, a * tile_cols : (a + n) * tile_cols]) for a, n in bounds
-    ]
-
-    small = jnp.dot(order, small, preferred_element_type=jnp.bfloat16)
+        exchange(jnp.concatenate([columns(0), proj_in[0], step_raw[0]], axis=1)),
+    ] + [exchange(columns(group)) for group in range(1, len(bounds))]
+    ahead = bounds[0][1] * tile_cols
+    small = jnp.dot(order, arrivals[0][:, ahead:], preferred_element_type=jnp.bfloat16)
     inputs = small[:, :state_size]
     readout = small[:, state_size : 2 * state_size]
     steps = jax.nn.softplus(small[:, 2 * state_size :].astype(jnp.float32))
@@ -231,7 +235,10 @@
     skip = jnp.repeat(head_skip_weight, head_size)[None, :]
 
     result = None
-    for (a, n), arrived in zip(bounds, arrivals):
+    for group, (a, n) in enumerate(bounds):
+        arrived = arrivals[group]
+        if result is not None:
+            arrived, result = lax.optimization_barrier((arrived, result))
         x, carried = states(order, arrived, inputs_t, factors, a, n, tile_cols)
         gathered = lax.all_gather(carried, "pos")
         result = outputs(

time: 425 us -> 394 us (0.927)
  local copies, waits for them, and re-layouts: 71.9 us -> 52.1 us
  waiting for transfers between devices: 223 us -> 235 us
  starting transfers between devices: 27.5 us -> 16 us
  matrix products: 25.6 us -> 19 us
    all_gather x5 -> x3, waiting for transfers between devices: 0.03 us -> 60 us  [on_device(): gathered = lax.all_gather(carried, 'pos')]
    all_to_all x6 -> x3, waiting for transfers between devices: 223 us -> 174 us  [exchange(): lax.all_to_all(packed, 'stream', split_axis=0, concat_axis=0, tiled=True)]
    unnamed x80 -> x74, local copies, waits for them, and re-layouts: 59.5 us -> 39.7 us
    all_to_all x6 -> x3, starting transfers between devices: 27.1 us -> 15.9 us  [exchange(): lax.all_to_all(packed, 'stream', split_axis=0, concat_axis=0, tiled=True)]
    dot_general x6 -> x3, matrix products: 24.7 us -> 16.7 us  [exchange(): packed = jnp.dot(pack, block, preferred_element_type=jnp.bfloat16)]
    pallas_call x5 -> x3, Pallas kernels: 22.2 us -> 19.8 us  [states(): pl.pallas_call(state_kernel, grid=(tiles,), in_specs=[pl.BlockSpec((rows,...]
    pallas_call x5 -> x3, Pallas kernels: 31.2 us -> 30.2 us  [outputs(): pl.pallas_call(output_kernel, grid=(tiles,), in_specs=in_specs, out_specs...]
  transfers between devices with their start and end apart: 11 -> 6, of which waited for: 6 -> 6; matrix products, arithmetic and copies ran while one was open for 9% -> 7% of each run, Pallas kernels for 12% -> 8%
where the time goes in v2:
time: 394 us; the launch traced here: 392 us
  waiting for transfers between devices  235 us (60%)
  local copies, waits for them, and re-layouts  52.1 us (13%)
  Pallas kernels  49.9 us (13%)
  matrix products  19 us (5%)
  starting transfers between devices  16 us (4%)
  between operations  13.4 us (3%)
  blocking collectives  5.21 us (1%)
    all_to_all x3, waiting for transfers between devices, exchange(): lax.all_to_all(packed, 'stream', split_axis=0, concat_axis=0, tiled=True)  174 us
    all_gather x3, waiting for transfers between devices, on_device(): gathered = lax.all_gather(carried, 'pos')  60 us
    unnamed x74, local copies, waits for them, and re-layouts  39.7 us
    pallas_call x3, Pallas kernels, outputs(): pl.pallas_call(output_kernel, grid=(tiles,), in_specs=in_specs, out_specs...  30.2 us
    pallas_call x3, Pallas kernels, states(): pl.pallas_call(state_kernel, grid=(tiles,), in_specs=[pl.BlockSpec((rows,...  19.8 us
    dot_general x3, matrix products, exchange(): packed = jnp.dot(pack, block, preferred_element_type=jnp.bfloat16)  16.7 us
    all_to_all x3, starting transfers between devices, exchange(): lax.all_to_all(packed, 'stream', split_axis=0, concat_axis=0, tiled=True)  15.9 us
    reshape x3, local copies, waits for them, and re-layouts, by_tile(): return jnp.moveaxis(array.reshape(rows, all_tiles, TILE_HEADS), 1, 0)  7.95 us
  transfers between devices with their start and end apart: 6, of which 6 were waited for; matrix products, arithmetic and copies ran while one was open for 7% of the time, Pallas kernels for 8%

profile of v2, /device:TPU:0, one launch (start us, length us, event | category | flops | bytes accessed | tf_op | source)
XLA Modules:
  0.0 392.4 jit_solution(17592788175230752732)
XLA Ops:
  10.1 4.1 %fusion.2 = bf16[768,2432]{1,0:T(8,128)(2,1)} fusion(bf16[512,128]{1,0:T(8,128)(2,1)S(1)} %bitcast.99, bf16[512,256]{1,0:T(8,128)(2,1)S(1)} %bitcast.98, bf16[512,2048]{1,0:T(8,128)(2,1)S(1)} %slice.42, s32[768]{0:T(1024)S(1)} %add.60), kind=kOutput, calls=%fused_computation.2 | convolution fusion | flops 1920466944 | bytes 6228992 | tf_op jit(solution)/shard_map/dot_general | solution.py:192
  14.2 7.3 %all-to-all-start.2 = ((bf16[8,96,2432]{2,1,0:T(8,128)(2,1)}), bf16[8,96,2432]{2,1,0:T(8,128)(2,1)}, u32[]{:S(2)}, u32[]{:S(2)}) async-start(bf16[8,96,2432]{2,1,0:T(8,128)(2,1)} %bitcast.84), calls=%async_computation.2 | async-start | bytes 7471104 | tf_op jit(solution)/shard_map/all_to_all | solution.py:194
  21.4 8.4 %fusion = bf16[768,4608]{1,0:T(8,128)(2,1)} fusion(bf16[512,8192]{1,0:T(8,128)(2,1)} %bitcast.91, s32[768]{0:T(1024)S(1)} %add.60), kind=kOutput, calls=%fused_computation | convolution fusion | flops 3624271872 | bytes 11799552 | tf_op jit(solution)/shard_map/dot_general | solution.py:192
  29.8 75.1 %all-to-all-done.2 = bf16[8,96,2432]{2,1,0:T(8,128)(2,1)} async-done(((bf16[8,96,2432]{2,1,0:T(8,128)(2,1)}), bf16[8,96,2432]{2,1,0:T(8,128)(2,1)}, u32[]{:S(2)}, u32[]{:S(2)}) %all-to-all-start.2) | async-done | bytes 3735584 | tf_op jit(solution)/shard_map/all_to_all | solution.py:194
  104.9 5.0 %all-to-all-start.1 = ((bf16[8,96,4608]{2,1,0:T(8,128)(2,1)}), bf16[8,96,4608]{2,1,0:T(8,128)(2,1)}, u32[]{:S(2)}, u32[]{:S(2)}) async-start(bf16[8,96,4608]{2,1,0:T(8,128)(2,1)} %bitcast.82), calls=%async_computation.1 | async-start | bytes 14155776 | tf_op jit(solution)/shard_map/all_to_all | solution.py:194
  111.4 1.9 fusion.10
  114.6 2.7 copy.26
  117.3 2.2 copy-done.6
  119.5 6.0 %shard_map.64 = (bf16[512,2048]{1,0:T(8,128)(2,1)S(1)}, bf16[128,2048]{1,0:T(8,128)(2,1)}) custom-call(bf16[512,768]{1,0:T(8,128)(2,1)S(1)} %fusion.11.order_ref, bf16[768,2432]{1,0:T(8,128)(2,1)} %bitcast.12.arrived_ref, bf16[128,512]{1,0:T(8,128)(2,1)S(1)} %get-tuple-element.28.inputs_t_ref, f32[16,512,8]{2,1,0:T(8,128)S(1)} %bitcast.76), custom_call_target="tpu_custom_call" | custom-call | flops 1879048192 | bytes 5767168 | tf_op jit(solution)/shard_map/pallas_call | solution.py:95
  127.1 2.6 copy.28
  129.8 2.7 copy.29
  132.4 5.2 %all-gather.3 = f32[4,1,128]{2,1,0:T(1,128)S(1)} all-gather(f32[1,1,128]{2,1,0:T(1,128)S(1)} %bitcast.96), channel_id=1, replica_groups=mesh['pos'=4,'stream'=8] {'pos'}, dimensions={0}, use_global_device_ids=true | all-gather | bytes 2560 | tf_op jit(solution)/shard_map/all_gather | solution.py:229
  138.5 12.4 %all-gather.8.cloned.1.call-done = bf16[512,2048]{1,0:T(8,128)(2,1)} async-done(((bf16[128,2048]{1,0:T(8,128)(2,1)}), bf16[512,2048]{1,0:T(8,128)(2,1)}) %all-gather.8.cloned.1.call-update) | async-done | bytes 2097168 | tf_op jit(solution)/shard_map/all_gather | solution.py:243
  150.9 2.2 copy-done
  153.1 2.2 copy-done.3
  158.5 7.6 %shard_map.65.rest_0_ = bf16[512,8192]{1,0:T(8,128)(2,1)} custom-call(bf16[512,2048]{1,0:T(8,128)(2,1)S(1)} %copy-done.19, f32[512,512]{1,0:T(8,128)S(1)} %fusion.21.scores_ref, bf16[512,128]{1,0:T(8,128)(2,1)S(1)} %copy.30.readout_ref, f32[16,512,8]{2,1,0:T(8,128)S(1)} %bitcast.70, f32[16,512,8]{2,1,0:T(8,128)S(1)} %bitcast.73, ...), custom_call_target="tpu_custom_call" | custom-call | flops 3489660928 | bytes 6291456 | tf_op jit(solution)/shard_map/pallas_call | solution.py:145
  166.1 97.9 %all-to-all-done.1 = bf16[8,96,4608]{2,1,0:T(8,128)(2,1)} async-done(((bf16[8,96,4608]{2,1,0:T(8,128)(2,1)}), bf16[8,96,4608]{2,1,0:T(8,128)(2,1)}, u32[]{:S(2)}, u32[]{:S(2)}) %all-to-all-start.1) | async-done | bytes 7077920 | tf_op jit(solution)/shard_map/all_to_all | solution.py:194
  264.0 2.2 copy-done.7
  266.2 10.6 %shard_map.66 = (bf16[512,4608]{1,0:T(8,128)(2,1)S(1)}, bf16[128,4608]{1,0:T(8,128)(2,1)S(1)}) custom-call(bf16[512,768]{1,0:T(8,128)(2,1)S(1)} %fusion.11.order_ref, bf16[768,4608]{1,0:T(8,128)(2,1)} %bitcast.8.arrived_ref, bf16[128,512]{1,0:T(8,128)(2,1)S(1)} %get-tuple-element.28.inputs_t_ref, f32[16,512,8]{2,1,0:T(8,128)S(1)} %bitcast.77), custom_call_target="tpu_custom_call" | custom-call | flops 4227858432 | bytes 12976128 | tf_op jit(solution)/shard_map/pallas_call | solution.py:95
  276.8 2.1 copy-done.11
  280.1 4.2 %fusion.8 = bf16[768,1536]{1,0:T(8,128)(2,1)} fusion(bf16[512,8192]{1,0:T(8,128)(2,1)} %bitcast.92, s32[768]{0:T(1024)S(1)} %add.60), kind=kOutput, calls=%fused_computation.8 | convolution fusion | flops 1208352768 | bytes 3935232 | tf_op jit(solution)/shard_map/dot_general | solution.py:192
  284.3 3.7 all-to-all-start
  288.0 28.8 %all-gather.10.cloned.1.call-done = bf16[512,4608]{1,0:T(8,128)(2,1)} async-done(((bf16[128,4608]{1,0:T(8,128)(2,1)}), bf16[512,4608]{1,0:T(8,128)(2,1)}) %all-gather.10.cloned.1.call-update) | async-done | bytes 4718608 | tf_op jit(solution)/shard_map/all_gather | solution.py:243
  316.8 2.2 copy-done.1
  319.0 2.2 copy-done.4
  323.8 16.7 %shard_map.67.rest_0_ = bf16[512,8192]{1,0:T(8,128)(2,1)} custom-call(bf16[512,4608]{1,0:T(8,128)(2,1)} %copy-done.11, f32[512,512]{1,0:T(8,128)S(1)} %fusion.21.scores_ref, bf16[512,128]{1,0:T(8,128)(2,1)S(1)} %copy-done.16, f32[16,512,8]{2,1,0:T(8,128)S(1)} %bitcast.71, f32[16,512,8]{2,1,0:T(8,128)S(1)} %bitcast.74, ...), custom_call_target="tpu_custom_call", output_to_operand_aliasing={{}: (9, {})} | custom-call | flops 7851737088 | bytes 14155776 | tf_op jit(solution)/shard_map/pallas_call | solution.py:145
  341.9 2.2 copy-done.8
  346.2 3.1 shard_map.68
  351.2 18.9 %all-gather.12.cloned.1.call-done = bf16[512,1536]{1,0:T(8,128)(2,1)} async-done(((bf16[128,1536]{1,0:T(8,128)(2,1)}), bf16[512,1536]{1,0:T(8,128)(2,1)}) %all-gather.12.cloned.1.call-update) | async-done | bytes 1572880 | tf_op jit(solution)/shard_map/all_gather | solution.py:243
  370.2 2.2 copy-done.2
  372.3 2.2 copy-done.5
  380.0 5.9 %shard_map.69 = bf16[512,8192]{1,0:T(8,128)(2,1)} custom-call(bf16[512,1536]{1,0:T(8,128)(2,1)S(1)} %copy-done.22, f32[512,512]{1,0:T(8,128)S(1)} %fusion.21.scores_ref, bf16[512,128]{1,0:T(8,128)(2,1)S(1)} %copy-done.17, f32[16,512,8]{2,1,0:T(8,128)S(1)} %bitcast.72, f32[16,512,8]{2,1,0:T(8,128)S(1)} %bitcast.75, ...), custom_call_target="tpu_custom_call", output_to_operand_aliasing={{}: (9, {})} | custom-call | flops 2617245696 | bytes 4718592 | tf_op jit(solution)/shard_map/pallas_call | solution.py:145
  (104 shorter events, 26.5 us)
Async XLA Ops:
  6.5 3.5 copy-start.33
  6.5 3.5 copy-start.32
  14.2 90.7 %all-to-all-start.2 = ((bf16[8,96,2432]{2,1,0:T(8,128)(2,1)}), bf16[8,96,2432]{2,1,0:T(8,128)(2,1)}, u32[]{:S(2)}, u32[]{:S(2)}) async-start(bf16[8,96,2432]{2,1,0:T(8,128)(2,1)} %bitcast.84), calls=%async_computation.2 | async-start | bytes 7471104 | tf_op jit(solution)/shard_map/all_to_all | solution.py:194
  104.9 6.2 %copy-start.34 = (f32[128]{0:T(128)S(1)}, f32[128]{0:T(128)}, u32[]{:S(2)}) copy-start(f32[128]{0:T(128)} %param.9) | copy-start | bytes 1540
  104.9 159.1 %all-to-all-start.1 = ((bf16[8,96,4608]{2,1,0:T(8,128)(2,1)}), bf16[8,96,4608]{2,1,0:T(8,128)(2,1)}, u32[]{:S(2)}, u32[]{:S(2)}) async-start(bf16[8,96,4608]{2,1,0:T(8,128)(2,1)} %bitcast.82), calls=%async_computation.1 | async-start | bytes 14155776 | tf_op jit(solution)/shard_map/all_to_all | solution.py:194
  109.9 41.0 %all-gather.8.cloned.1.call-start = ((), (), s32[]{:S(2)}) async-start(), calls=%async_computation.3 | async-start | bytes 2621440 | tf_op jit(solution)/shard_map/all_gather | solution.py:243
  111.4 152.6 %copy-start.9 = (bf16[512,768]{1,0:T(8,128)(2,1)}, bf16[512,768]{1,0:T(8,128)(2,1)S(1)}, u32[]{:S(2)}) copy-start(bf16[512,768]{1,0:T(8,128)(2,1)S(1)} %fusion.11.order_ref) | copy-start | bytes 2359300
  114.6 36.3 %copy-start.12 = (f32[16,8,512]{2,1,0:T(8,128)}, f32[16,8,512]{2,1,0:T(8,128)S(1)}, u32[]{:S(2)}) copy-start(f32[16,8,512]{2,1,0:T(8,128)S(1)} %get-tuple-element.25.source_ref) | copy-start | bytes 786436
  117.3 146.7 %copy-start.24 = (bf16[128,512]{1,0:T(8,128)(2,1)}, bf16[128,512]{1,0:T(8,128)(2,1)S(1)}, u32[]{:S(2)}) copy-start(bf16[128,512]{1,0:T(8,128)(2,1)S(1)} %get-tuple-element.28.inputs_t_ref) | copy-start | bytes 393220
  117.3 2.2 copy-start.6
  119.5 7.4 %copy-start.31 = (f32[128]{0:T(128)S(1)}, f32[128]{0:T(128)}, u32[]{:S(2)}) copy-start(f32[128]{0:T(128)} %param.10) | copy-start | bytes 1540
  125.5 1.3 copy-start.18
  126.9 189.9 %all-gather.10.cloned.1.call-start = ((), (), s32[]{:S(2)}) async-start(), calls=%async_computation.4 | async-start | bytes 5898240 | tf_op jit(solution)/shard_map/all_gather | solution.py:243
  127.1 23.8 %copy-start.27 = (f32[1,8192]{1,0:T(1,128)}, f32[1,8192]{1,0:T(1,128)S(1)}, u32[]{:S(2)}) copy-start(f32[1,8192]{1,0:T(1,128)S(1)} %broadcast_in_dim_reshape.2.skip_ref) | copy-start | bytes 98308
  138.2 27.9 %copy-start.15 = (bf16[512,128]{1,0:T(8,128)(2,1)}, bf16[512,128]{1,0:T(8,128)(2,1)S(1)}, u32[]{:S(2)}) copy-start(bf16[512,128]{1,0:T(8,128)(2,1)S(1)} %copy.30.readout_ref) | copy-start | bytes 393220
  150.9 2.2 copy-start
  153.1 2.2 copy-start.3
  155.3 1.6 copy-start.19
  156.9 1.6 copy-start.20
  264.0 2.2 copy-start.7
  276.8 2.1 copy-start.11
  284.3 57.6 %all-to-all-start = ((bf16[8,96,1536]{2,1,0:T(8,128)(2,1)}), bf16[8,96,1536]{2,1,0:T(8,128)(2,1)S(1)}, u32[]{:S(2)}, u32[]{:S(2)}) async-start(bf16[8,96,1536]{2,1,0:T(8,128)(2,1)} %bitcast.85), calls=%async_computation | async-start | bytes 4718592 | tf_op jit(solution)/shard_map/all_to_all | solution.py:194
  288.0 82.2 %all-gather.12.cloned.1.call-start = ((), (), s32[]{:S(2)}) async-start(), calls=%async_computation.5 | async-start | bytes 1966080 | tf_op jit(solution)/shard_map/all_gather | solution.py:243
  316.8 2.2 copy-start.1
  319.0 2.2 copy-start.4
  341.9 2.2 copy-start.8
  344.1 1.1 copy-start.10
  349.3 1.2 copy-start.21
  370.2 2.2 copy-start.2
  372.3 2.2 copy-start.5
  376.4 1.4 copy-start.22
  377.8 1.4 copy-start.23
  (9 other events, 8.0 us)
Sparse Core Ops, SparseCore 0:
  127.0 23.8 all-gather.7
  280.2 36.5 all-gather.9
  351.4 18.7 all-gather.11

commit v3 on v2

--- a/solution.py
+++ b/solution.py
@@ -7,9 +7,9 @@
 
 TILE_HEADS = 8
 ROWS = 128
-GROUPS = (4, 9, 3)
+GROUPS = (5, 8, 3)
 LOG2E = 1.4426950408889634
-VMEM = 40 * 1024 * 1024
+VMEM = 58 * 1024 * 1024
 
 
 def expand(factors, pair, low):
@@ -237,7 +237,7 @@
     result = None
     for group, (a, n) in enumerate(bounds):
         arrived = arrivals[group]
-        if result is not None:
+        if result is not None and group + 1 < len(bounds):
             arrived, result = lax.optimization_barrier((arrived, result))
         x, carried = states(order, arrived, inputs_t, factors, a, n, tile_cols)
         gathered = lax.all_gather(carried, "pos")

time: 394 us -> 376 us (0.954)
  blocking collectives: 5.21 us -> 62.7 us
  waiting for transfers between devices: 235 us -> 191 us
  local copies, waits for them, and re-layouts: 52.1 us -> 15.2 us
  Pallas kernels: 49.9 us -> 58.1 us
    all_to_all x0 -> x1, blocking collectives: none -> 57.7 us  [exchange(): lax.all_to_all(packed, 'stream', split_axis=0, concat_axis=0, tiled=True)]
    all_gather x3, waiting for transfers between devices: 60 us -> 15.8 us  [on_device(): gathered = lax.all_gather(carried, 'pos')]
    unnamed x74 -> x12, local copies, waits for them, and re-layouts: 39.7 us -> 1.45 us
    pallas_call x3, Pallas kernels: 19.8 us -> 23.9 us  [states(): pl.pallas_call(state_kernel, grid=(tiles,), in_specs=[pl.BlockSpec((rows,...]
    pallas_call x3, Pallas kernels: 30.2 us -> 34.2 us  [outputs(): pl.pallas_call(output_kernel, grid=(tiles,), in_specs=in_specs, out_specs...]
    all_to_all x3 -> x2, starting transfers between devices: 15.9 us -> 12.1 us  [exchange(): lax.all_to_all(packed, 'stream', split_axis=0, concat_axis=0, tiled=True)]
    all_to_all x3 -> x2, waiting for transfers between devices: 174 us -> 175 us  [exchange(): lax.all_to_all(packed, 'stream', split_axis=0, concat_axis=0, tiled=True)]
  transfers between devices with their start and end apart: 6 -> 5, of which waited for: 6 -> 4; matrix products, arithmetic and copies ran while one was open for 7% -> 8% of each run, Pallas kernels for 8% -> 11%
where the time goes in v3:
time: 376 us; the launch traced here: 375 us
  waiting for transfers between devices  191 us (51%)
  blocking collectives  62.7 us (17%)
  Pallas kernels  58.1 us (15%)
  matrix products  18 us (5%)
  local copies, waits for them, and re-layouts  15.2 us (4%)
  between operations  13.2 us (4%)
  starting transfers between devices  12.3 us (3%)
  other arithmetic  3.81 us (1%)
    all_to_all x2, waiting for transfers between devices, exchange(): lax.all_to_all(packed, 'stream', split_axis=0, concat_axis=0, tiled=True)  175 us
    all_to_all x1, blocking collectives, exchange(): lax.all_to_all(packed, 'stream', split_axis=0, concat_axis=0, tiled=True)  57.7 us
    pallas_call x3, Pallas kernels, outputs(): pl.pallas_call(output_kernel, grid=(tiles,), in_specs=in_specs, out_specs...  34.2 us
    pallas_call x3, Pallas kernels, states(): pl.pallas_call(state_kernel, grid=(tiles,), in_specs=[pl.BlockSpec((rows,...  23.9 us
    all_gather x3, waiting for transfers between devices, on_device(): gathered = lax.all_gather(carried, 'pos')  15.8 us
    dot_general x3, matrix products, exchange(): packed = jnp.dot(pack, block, preferred_element_type=jnp.bfloat16)  15 us
    all_to_all x2, starting transfers between devices, exchange(): lax.all_to_all(packed, 'stream', split_axis=0, concat_axis=0, tiled=True)  12.1 us
    reshape x3, local copies, waits for them, and re-layouts, by_tile(): return jnp.moveaxis(array.reshape(rows, all_tiles, TILE_HEADS), 1, 0)  7.77 us
  transfers between devices with their start and end apart: 5, of which 4 were waited for; matrix products, arithmetic and copies ran while one was open for 8% of the time, Pallas kernels for 11%

profile of v3, /device:TPU:0, one launch (start us, length us, event | category | flops | bytes accessed | tf_op | source)
XLA Modules:
  0.0 374.5 jit_solution(8608120166156905122)
XLA Ops:
  6.5 0.7 fusion.25
  7.5 0.7 bitcast_subtract_fusion
  8.3 1.9 slice.41
  10.2 4.6 %fusion.2 = bf16[768,2944]{1,0:T(8,128)(2,1)} fusion(bf16[512,128]{1,0:T(8,128)(2,1)S(1)} %bitcast.99, bf16[512,256]{1,0:T(8,128)(2,1)S(1)} %bitcast.98, bf16[512,2560]{1,0:T(8,128)(2,1)S(1)} %slice.41, s32[768]{0:T(1024)S(1)} %add.60), kind=kOutput, calls=%fused_computation.2 | convolution fusion | flops 2324692992 | bytes 7539712 | tf_op jit(solution)/shard_map/dot_general | solution.py:192
  14.8 7.3 %all-to-all-start.1 = ((bf16[8,96,2944]{2,1,0:T(8,128)(2,1)}), bf16[8,96,2944]{2,1,0:T(8,128)(2,1)}, u32[]{:S(2)}, u32[]{:S(2)}) async-start(bf16[8,96,2944]{2,1,0:T(8,128)(2,1)} %bitcast.81), calls=%async_computation.1 | async-start | bytes 9043968 | tf_op jit(solution)/shard_map/all_to_all | solution.py:194
  22.1 7.6 %fusion = bf16[768,4096]{1,0:T(8,128)(2,1)} fusion(bf16[512,8192]{1,0:T(8,128)(2,1)} %bitcast.91, s32[768]{0:T(1024)S(1)} %add.60), kind=kOutput, calls=%fused_computation | convolution fusion | flops 3221618688 | bytes 10488832 | tf_op jit(solution)/shard_map/dot_general | solution.py:192
  29.7 92.7 %all-to-all-done.1 = bf16[8,96,2944]{2,1,0:T(8,128)(2,1)} async-done(((bf16[8,96,2944]{2,1,0:T(8,128)(2,1)}), bf16[8,96,2944]{2,1,0:T(8,128)(2,1)}, u32[]{:S(2)}, u32[]{:S(2)}) %all-to-all-start.1) | async-done | bytes 4522016 | tf_op jit(solution)/shard_map/all_to_all | solution.py:194
  122.4 4.9 %all-to-all-start.2 = ((bf16[8,96,4096]{2,1,0:T(8,128)(2,1)}), bf16[8,96,4096]{2,1,0:T(8,128)(2,1)}, u32[]{:S(2)}, u32[]{:S(2)}) async-start(bf16[8,96,4096]{2,1,0:T(8,128)(2,1)} %bitcast.80), calls=%async_computation.2 | async-start | bytes 12582912 | tf_op jit(solution)/shard_map/all_to_all | solution.py:194
  127.3 0.9 dynamic-slice_reduce_fusion
  128.6 1.1 fusion.11.order_ref
  129.7 1.6 fusion.10
  132.3 1.0 subtract_bitcast_fusion
  133.3 2.6 copy.26
  135.9 0.7 fusion.27
  136.6 7.6 %shard_map.65 = (bf16[512,2560]{1,0:T(8,128)(2,1)}, bf16[128,2560]{1,0:T(8,128)(2,1)}) custom-call(bf16[512,768]{1,0:T(8,128)(2,1)} %fusion.11.order_ref, bf16[768,2944]{1,0:T(8,128)(2,1)} %bitcast.10.arrived_ref, bf16[128,512]{1,0:T(8,128)(2,1)} %get-tuple-element.24.inputs_t_ref, f32[16,512,8]{2,1,0:T(8,128)} %bitcast.76), custom_call_target="tpu_custom_call" | custom-call | flops 2348810240 | bytes 7208960 | tf_op jit(solution)/shard_map/pallas_call | solution.py:95
  144.3 0.7 broadcast_in_dim_reshape.2.skip_ref
  145.0 0.7 copy.30.readout_ref
  145.8 2.6 copy.28
  148.3 2.6 copy.29
  150.9 5.0 %all-gather.3 = f32[4,1,128]{2,1,0:T(1,128)S(1)} all-gather(f32[1,1,128]{2,1,0:T(1,128)S(1)} %bitcast.96), channel_id=1, replica_groups=mesh['pos'=4,'stream'=8] {'pos'}, dimensions={0}, use_global_device_ids=true | all-gather | bytes 2560 | tf_op jit(solution)/shard_map/all_gather | solution.py:229
  156.2 0.8 reshape.205.coef_ref
  157.0 1.3 fusion.21.scores_ref
  158.3 12.8 %all-gather.10.cloned.1.call-done = bf16[512,2560]{1,0:T(8,128)(2,1)} async-done(((bf16[128,2560]{1,0:T(8,128)(2,1)}), bf16[512,2560]{1,0:T(8,128)(2,1)}) %all-gather.10.cloned.1.call-update) | async-done | bytes 2621456 | tf_op jit(solution)/shard_map/all_gather | solution.py:243
  171.2 10.8 %shard_map.66.rest_0_ = bf16[512,8192]{1,0:T(8,128)(2,1)} custom-call(bf16[512,2560]{1,0:T(8,128)(2,1)} %get-tuple-element.15.x_ref, f32[512,512]{1,0:T(8,128)} %fusion.21.scores_ref, bf16[512,128]{1,0:T(8,128)(2,1)} %copy.30.readout_ref, f32[16,512,8]{2,1,0:T(8,128)} %bitcast.70, f32[16,512,8]{2,1,0:T(8,128)} %bitcast.73, ...), custom_call_target="tpu_custom_call" | custom-call | flops 4362076160 | bytes 7864320 | tf_op jit(solution)/shard_map/pallas_call | solution.py:145
  182.0 82.6 %all-to-all-done.2 = bf16[8,96,4096]{2,1,0:T(8,128)(2,1)} async-done(((bf16[8,96,4096]{2,1,0:T(8,128)(2,1)}), bf16[8,96,4096]{2,1,0:T(8,128)(2,1)}, u32[]{:S(2)}, u32[]{:S(2)}) %all-to-all-start.2) | async-done | bytes 6291488 | tf_op jit(solution)/shard_map/all_to_all | solution.py:194
  264.6 11.0 %shard_map.67 = (bf16[512,4096]{1,0:T(8,128)(2,1)}, bf16[128,4096]{1,0:T(8,128)(2,1)}) custom-call(bf16[512,768]{1,0:T(8,128)(2,1)} %fusion.11.order_ref, bf16[768,4096]{1,0:T(8,128)(2,1)} %bitcast.26.arrived_ref, bf16[128,512]{1,0:T(8,128)(2,1)} %get-tuple-element.24.inputs_t_ref, f32[16,512,8]{2,1,0:T(8,128)} %bitcast.77), custom_call_target="tpu_custom_call" | custom-call | flops 3758096384 | bytes 11534336 | tf_op jit(solution)/shard_map/pallas_call | solution.py:95
  275.7 2.8 fusion.8
  278.5 57.7 %all_to_all.15 = bf16[8,96,1536]{2,1,0:T(8,128)(2,1)} all-to-all(bf16[8,96,1536]{2,1,0:T(8,128)(2,1)S(1)} %bitcast.84), channel_id=1, replica_groups=mesh['pos'=4,'stream'=8] {'stream'}, dimensions={0} | all-to-all | bytes 4718592 | tf_op jit(solution)/shard_map/all_to_all | solution.py:194
  336.2 5.4 %shard_map.64 = (bf16[512,1536]{1,0:T(8,128)(2,1)}, bf16[128,1536]{1,0:T(8,128)(2,1)}) custom-call(bf16[512,768]{1,0:T(8,128)(2,1)} %fusion.11.order_ref, bf16[768,1536]{1,0:T(8,128)(2,1)} %bitcast.79, bf16[128,512]{1,0:T(8,128)(2,1)} %get-tuple-element.24.inputs_t_ref, f32[16,512,8]{2,1,0:T(8,128)} %bitcast.78), custom_call_target="tpu_custom_call" | custom-call | flops 1409286144 | bytes 4325376 | tf_op jit(solution)/shard_map/pallas_call | solution.py:95
  341.6 15.8 %shard_map.68.rest_0_ = bf16[512,8192]{1,0:T(8,128)(2,1)} custom-call(bf16[512,4096]{1,0:T(8,128)(2,1)} %get-tuple-element.18.x_ref, f32[512,512]{1,0:T(8,128)} %fusion.21.scores_ref, bf16[512,128]{1,0:T(8,128)(2,1)} %copy.30.readout_ref, f32[16,512,8]{2,1,0:T(8,128)} %bitcast.71, f32[16,512,8]{2,1,0:T(8,128)} %bitcast.74, ...), custom_call_target="tpu_custom_call", output_to_operand_aliasing={{}: (9, {})} | custom-call | flops 6979321856 | bytes 12582912 | tf_op jit(solution)/shard_map/pallas_call | solution.py:145
  357.4 3.0 all-gather.8.cloned.1.call-done
  360.4 7.5 %shard_map.69 = bf16[512,8192]{1,0:T(8,128)(2,1)} custom-call(bf16[512,1536]{1,0:T(8,128)(2,1)} %get-tuple-element.13.x_ref, f32[512,512]{1,0:T(8,128)} %fusion.21.scores_ref, bf16[512,128]{1,0:T(8,128)(2,1)} %copy.30.readout_ref, f32[16,512,8]{2,1,0:T(8,128)} %bitcast.72, f32[16,512,8]{2,1,0:T(8,128)} %bitcast.75, ...), custom_call_target="tpu_custom_call", output_to_operand_aliasing={{}: (9, {})} | custom-call | flops 2617245696 | bytes 4718592 | tf_op jit(solution)/shard_map/pallas_call | solution.py:145
  (41 shorter events, 2.2 us)
Async XLA Ops:
  6.5 3.7 copy-start.2
  6.5 3.7 copy-start.1
  14.8 107.6 %all-to-all-start.1 = ((bf16[8,96,2944]{2,1,0:T(8,128)(2,1)}), bf16[8,96,2944]{2,1,0:T(8,128)(2,1)}, u32[]{:S(2)}, u32[]{:S(2)}) async-start(bf16[8,96,2944]{2,1,0:T(8,128)(2,1)} %bitcast.81), calls=%async_computation.1 | async-start | bytes 9043968 | tf_op jit(solution)/shard_map/all_to_all | solution.py:194
  122.4 6.2 %copy-start.3 = (f32[128]{0:T(128)S(1)}, f32[128]{0:T(128)}, u32[]{:S(2)}) copy-start(f32[128]{0:T(128)} %param.9) | copy-start | bytes 1540
  122.4 142.2 %all-to-all-start.2 = ((bf16[8,96,4096]{2,1,0:T(8,128)(2,1)}), bf16[8,96,4096]{2,1,0:T(8,128)(2,1)}, u32[]{:S(2)}, u32[]{:S(2)}) async-start(bf16[8,96,4096]{2,1,0:T(8,128)(2,1)} %bitcast.80), calls=%async_computation.2 | async-start | bytes 12582912 | tf_op jit(solution)/shard_map/all_to_all | solution.py:194
  127.3 43.9 %all-gather.10.cloned.1.call-start = ((), (), s32[]{:S(2)}) async-start(), calls=%async_computation.4 | async-start | bytes 3276800 | tf_op jit(solution)/shard_map/all_gather | solution.py:243
  136.6 7.6 %copy-start = (f32[128]{0:T(128)S(1)}, f32[128]{0:T(128)}, u32[]{:S(2)}) copy-start(f32[128]{0:T(128)} %param.10) | copy-start | bytes 1540
  144.1 197.5 %all-gather.12.cloned.1.call-start = ((), (), s32[]{:S(2)}) async-start(), calls=%async_computation.5 | async-start | bytes 5242880 | tf_op jit(solution)/shard_map/all_gather | solution.py:243
  275.6 84.8 %all-gather.8.cloned.1.call-start = ((), (), s32[]{:S(2)}) async-start(), calls=%async_computation.3 | async-start | bytes 1966080 | tf_op jit(solution)/shard_map/all_gather | solution.py:243
Sparse Core Ops, SparseCore 0:
  144.3 26.8 all-gather.9
  275.7 33.5 all-gather.11
  341.7 18.6 all-gather.7

commit v4 on v3

--- a/solution.py
+++ b/solution.py
@@ -7,7 +7,7 @@
 
 TILE_HEADS = 8
 ROWS = 128
-GROUPS = (5, 8, 3)
+GROUPS = (7, 8, 1)
 LOG2E = 1.4426950408889634
 VMEM = 58 * 1024 * 1024
 
@@ -188,11 +188,14 @@
     ).reshape(slots)
     order = (position[:, None] == landed[None, :]).astype(jnp.bfloat16)
 
+    def packed(block):
+        return jnp.dot(pack, block, preferred_element_type=jnp.bfloat16)
+
     def exchange(block):
-        packed = jnp.dot(pack, block, preferred_element_type=jnp.bfloat16)
-        packed = packed.reshape(streams, capacity, block.shape[1])
-        arrived = lax.all_to_all(packed, "stream", split_axis=0, concat_axis=0, tiled=True)
-        return arrived.reshape(slots, block.shape[1])
+        width = block.shape[1]
+        block = block.reshape(streams, capacity, width)
+        arrived = lax.all_to_all(block, "stream", split_axis=0, concat_axis=0, tiled=True)
+        return arrived.reshape(slots, width)
 
     bounds = []
     first = 0
@@ -205,9 +208,9 @@
         a, n = bounds[group]
         return tokens[:, a * tile_cols : (a + n) * tile_cols]
 
-    arrivals = [
-        exchange(jnp.concatenate([columns(0), proj_in[0], step_raw[0]], axis=1)),
-    ] + [exchange(columns(group)) for group in range(1, len(bounds))]
+    leading = packed(jnp.concatenate([columns(0), proj_in[0], step_raw[0]], axis=1))
+    later = lax.optimization_barrier([packed(columns(g)) for g in range(1, len(bounds))])
+    arrivals = [exchange(block) for block in [leading, *later]]
     ahead = bounds[0][1] * tile_cols
     small = jnp.dot(order, arrivals[0][:, ahead:], preferred_element_type=jnp.bfloat16)
     inputs = small[:, :state_size]

time: 376 us -> 375 us (level)
  blocking collectives: 62.7 us -> 38.1 us
  waiting for transfers between devices: 191 us -> 215 us
    all_to_all x1, blocking collectives: 57.7 us -> 23.8 us  [exchange(): lax.all_to_all(block, 'stream', split_axis=0, concat_axis=0, tiled=True)]
    all_to_all x2, waiting for transfers between devices: 175 us -> 196 us  [exchange(): lax.all_to_all(block, 'stream', split_axis=0, concat_axis=0, tiled=True)]
    all_gather x0 -> x1, blocking collectives: none -> 9.33 us  [on_device(): gathered = lax.all_gather(carried, 'pos')]
    all_gather x3 -> x2, waiting for transfers between devices: 15.8 us -> 18.8 us  [on_device(): gathered = lax.all_gather(carried, 'pos')]
  transfers between devices with their start and end apart: 5 -> 4, of which waited for: 4 -> 3; matrix products, arithmetic and copies ran while one was open for 8% -> 7% of each run, Pallas kernels for 11% -> 7%
where the time goes in v4:
time: 375 us; the launch traced here: 374 us
  waiting for transfers between devices  215 us (57%)
  Pallas kernels  57.9 us (15%)
  blocking collectives  38.1 us (10%)
  matrix products  17.9 us (5%)
  local copies, waits for them, and re-layouts  15.6 us (4%)
  between operations  13.5 us (4%)
  starting transfers between devices  12.2 us (3%)
  other arithmetic  3.83 us (1%)
    all_to_all x2, waiting for transfers between devices, exchange(): lax.all_to_all(block, 'stream', split_axis=0, concat_axis=0, tiled=True)  196 us
    pallas_call x3, Pallas kernels, outputs(): pl.pallas_call(output_kernel, grid=(tiles,), in_specs=in_specs, out_specs...  34 us
    pallas_call x3, Pallas kernels, states(): pl.pallas_call(state_kernel, grid=(tiles,), in_specs=[pl.BlockSpec((rows,...  23.9 us
    all_to_all x1, blocking collectives, exchange(): lax.all_to_all(block, 'stream', split_axis=0, concat_axis=0, tiled=True)  23.8 us
    all_gather x2, waiting for transfers between devices, on_device(): gathered = lax.all_gather(carried, 'pos')  18.8 us
    dot_general x3, matrix products, packed(): return jnp.dot(pack, block, preferred_element_type=jnp.bfloat16)  15 us
    all_to_all x2, starting transfers between devices, exchange(): lax.all_to_all(block, 'stream', split_axis=0, concat_axis=0, tiled=True)  12.1 us
    all_gather x1, blocking collectives, on_device(): gathered = lax.all_gather(carried, 'pos')  9.33 us
  transfers between devices with their start and end apart: 4, of which 3 were waited for; matrix products, arithmetic and copies ran while one was open for 7% of the time, Pallas kernels for 7%

profile of v4, /device:TPU:0, one launch (start us, length us, event | category | flops | bytes accessed | tf_op | source)
XLA Modules:
  0.0 373.8 jit_solution(6067003063981294924)
XLA Ops:
  6.5 0.7 fusion.25
  7.5 0.7 bitcast_subtract_fusion
  8.3 2.3 slice.42
  10.6 5.7 %fusion.2 = bf16[768,3968]{1,0:T(8,128)(2,1)} fusion(bf16[512,128]{1,0:T(8,128)(2,1)S(1)} %bitcast.99, bf16[512,256]{1,0:T(8,128)(2,1)S(1)} %bitcast.98, bf16[512,3584]{1,0:T(8,128)(2,1)S(1)} %slice.42, s32[768]{0:T(1024)S(1)} %add.60), kind=kOutput, calls=%fused_computation.2 | convolution fusion | flops 3133145088 | bytes 10161152 | tf_op jit(solution)/shard_map/dot_general | solution.py:192
  16.3 7.3 %all-to-all-start.1 = ((bf16[8,96,3968]{2,1,0:T(8,128)(2,1)}), bf16[8,96,3968]{2,1,0:T(8,128)(2,1)}, u32[]{:S(2)}, u32[]{:S(2)}) async-start(bf16[8,96,3968]{2,1,0:T(8,128)(2,1)} %bitcast.80), calls=%async_computation.1 | async-start | bytes 12189696 | tf_op jit(solution)/shard_map/all_to_all | solution.py:197
  23.6 1.7 fusion.8
  25.2 7.6 %fusion = bf16[768,4096]{1,0:T(8,128)(2,1)} fusion(bf16[512,8192]{1,0:T(8,128)(2,1)} %bitcast.88, s32[768]{0:T(1024)S(1)} %add.60), kind=kOutput, calls=%fused_computation | convolution fusion | flops 3221618688 | bytes 10488832 | tf_op jit(solution)/shard_map/dot_general | solution.py:192
  32.8 124.8 %all-to-all-done.1 = bf16[8,96,3968]{2,1,0:T(8,128)(2,1)} async-done(((bf16[8,96,3968]{2,1,0:T(8,128)(2,1)}), bf16[8,96,3968]{2,1,0:T(8,128)(2,1)}, u32[]{:S(2)}, u32[]{:S(2)}) %all-to-all-start.1) | async-done | bytes 6094880 | tf_op jit(solution)/shard_map/all_to_all | solution.py:197
  157.6 4.9 %all-to-all-start.2 = ((bf16[8,96,4096]{2,1,0:T(8,128)(2,1)}), bf16[8,96,4096]{2,1,0:T(8,128)(2,1)}, u32[]{:S(2)}, u32[]{:S(2)}) async-start(bf16[8,96,4096]{2,1,0:T(8,128)(2,1)} %bitcast.79), calls=%async_computation.2 | async-start | bytes 12582912 | tf_op jit(solution)/shard_map/all_to_all | solution.py:197
  162.5 0.9 dynamic-slice_reduce_fusion
  163.7 1.1 fusion.10.order_ref
  164.8 1.6 fusion.9
  167.5 1.0 subtract_bitcast_fusion
  168.5 2.6 copy.26
  171.1 0.7 fusion.27
  171.8 9.8 %shard_map.65 = (bf16[512,3584]{1,0:T(8,128)(2,1)}, bf16[128,3584]{1,0:T(8,128)(2,1)}) custom-call(bf16[512,768]{1,0:T(8,128)(2,1)} %fusion.10.order_ref, bf16[768,3968]{1,0:T(8,128)(2,1)} %bitcast.10.arrived_ref, bf16[128,512]{1,0:T(8,128)(2,1)} %get-tuple-element.28.inputs_t_ref, f32[16,512,8]{2,1,0:T(8,128)} %bitcast.76), custom_call_target="tpu_custom_call" | custom-call | flops 3288334336 | bytes 10092544 | tf_op jit(solution)/shard_map/pallas_call | solution.py:95
  181.7 0.7 broadcast_in_dim_reshape.2.skip_ref
  182.5 0.8 copy.30.readout_ref
  183.2 2.6 copy.28
  185.8 2.6 copy.29
  188.4 5.0 %all-gather.3 = f32[4,1,128]{2,1,0:T(1,128)S(1)} all-gather(f32[1,1,128]{2,1,0:T(1,128)S(1)} %bitcast.95), channel_id=1, replica_groups=mesh['pos'=4,'stream'=8] {'pos'}, dimensions={0}, use_global_device_ids=true | all-gather | bytes 2560 | tf_op jit(solution)/shard_map/all_gather | solution.py:232
  193.7 0.8 reshape.205.coef_ref
  194.5 1.3 fusion.21.scores_ref
  195.8 18.8 %all-gather.7.cloned.1.call-done = bf16[512,3584]{1,0:T(8,128)(2,1)} async-done(((bf16[128,3584]{1,0:T(8,128)(2,1)}), bf16[512,3584]{1,0:T(8,128)(2,1)}) %all-gather.7.cloned.1.call-update) | async-done | bytes 3670032 | tf_op jit(solution)/shard_map/all_gather | solution.py:246
  214.6 14.1 %shard_map.66.rest_0_ = bf16[512,8192]{1,0:T(8,128)(2,1)} custom-call(bf16[512,3584]{1,0:T(8,128)(2,1)} %get-tuple-element.19.x_ref, f32[512,512]{1,0:T(8,128)} %fusion.21.scores_ref, bf16[512,128]{1,0:T(8,128)(2,1)} %copy.30.readout_ref, f32[16,512,8]{2,1,0:T(8,128)} %bitcast.70, f32[16,512,8]{2,1,0:T(8,128)} %bitcast.73, ...), custom_call_target="tpu_custom_call" | custom-call | flops 6106906624 | bytes 11010048 | tf_op jit(solution)/shard_map/pallas_call | solution.py:145
  228.6 71.1 %all-to-all-done.2 = bf16[8,96,4096]{2,1,0:T(8,128)(2,1)} async-done(((bf16[8,96,4096]{2,1,0:T(8,128)(2,1)}), bf16[8,96,4096]{2,1,0:T(8,128)(2,1)}, u32[]{:S(2)}, u32[]{:S(2)}) %all-to-all-start.2) | async-done | bytes 6291488 | tf_op jit(solution)/shard_map/all_to_all | solution.py:197
  299.8 11.0 %shard_map.67 = (bf16[512,4096]{1,0:T(8,128)(2,1)}, bf16[128,4096]{1,0:T(8,128)(2,1)}) custom-call(bf16[512,768]{1,0:T(8,128)(2,1)} %fusion.10.order_ref, bf16[768,4096]{1,0:T(8,128)(2,1)} %bitcast.26.arrived_ref, bf16[128,512]{1,0:T(8,128)(2,1)} %get-tuple-element.28.inputs_t_ref, f32[16,512,8]{2,1,0:T(8,128)} %bitcast.77), custom_call_target="tpu_custom_call" | custom-call | flops 3758096384 | bytes 11534336 | tf_op jit(solution)/shard_map/pallas_call | solution.py:95
  310.8 23.8 %all_to_all.15 = bf16[8,96,512]{2,1,0:T(8,128)(2,1)} all-to-all(bf16[8,96,512]{2,1,0:T(8,128)(2,1)S(1)} %bitcast.91), channel_id=1, replica_groups=mesh['pos'=4,'stream'=8] {'stream'}, dimensions={0} | all-to-all | bytes 1572864 | tf_op jit(solution)/shard_map/all_to_all | solution.py:197
  334.6 3.1 shard_map.64
  337.7 9.3 %all-gather = bf16[512,512]{1,0:T(8,128)(2,1)} all-gather(bf16[128,512]{1,0:T(8,128)(2,1)} %get-tuple-element.17), channel_id=2, replica_groups=mesh['pos'=4,'stream'=8] {'pos'}, dimensions={0}, use_global_device_ids=true | all-gather | bytes 655360 | tf_op jit(solution)/shard_map/all_gather | solution.py:246
  347.0 15.8 %shard_map.68.rest_0_ = bf16[512,8192]{1,0:T(8,128)(2,1)} custom-call(bf16[512,4096]{1,0:T(8,128)(2,1)} %get-tuple-element.22.x_ref, f32[512,512]{1,0:T(8,128)} %fusion.21.scores_ref, bf16[512,128]{1,0:T(8,128)(2,1)} %copy.30.readout_ref, f32[16,512,8]{2,1,0:T(8,128)} %bitcast.71, f32[16,512,8]{2,1,0:T(8,128)} %bitcast.74, ...), custom_call_target="tpu_custom_call", output_to_operand_aliasing={{}: (9, {})} | custom-call | flops 6979321856 | bytes 12582912 | tf_op jit(solution)/shard_map/pallas_call | solution.py:145
  362.8 4.1 %shard_map.69 = bf16[512,8192]{1,0:T(8,128)(2,1)} custom-call(bf16[512,512]{1,0:T(8,128)(2,1)} %get-tuple-element.16.x_ref, f32[512,512]{1,0:T(8,128)} %fusion.21.scores_ref, bf16[512,128]{1,0:T(8,128)(2,1)} %copy.30.readout_ref, f32[16,512,8]{2,1,0:T(8,128)} %bitcast.72, f32[16,512,8]{2,1,0:T(8,128)} %bitcast.75, ...), custom_call_target="tpu_custom_call", output_to_operand_aliasing={{}: (9, {})} | custom-call | flops 872415232 | bytes 1572864 | tf_op jit(solution)/shard_map/pallas_call | solution.py:145
  (39 shorter events, 2.1 us)
Async XLA Ops:
  6.5 4.1 %copy-start.2 = (bf16[1,512,128]{2,1,0:T(8,128)(2,1)S(1)}, bf16[1,512,128]{2,1,0:T(8,128)(2,1)}, u32[]{:S(2)}) copy-start(bf16[1,512,128]{2,1,0:T(8,128)(2,1)} %param.8) | copy-start | bytes 393220
  6.5 4.1 %copy-start.1 = (bf16[1,512,256]{2,1,0:T(8,128)(2,1)S(1)}, bf16[1,512,256]{2,1,0:T(8,128)(2,1)}, u32[]{:S(2)}) copy-start(bf16[1,512,256]{2,1,0:T(8,128)(2,1)} %param.7) | copy-start | bytes 786436
  16.3 141.3 %all-to-all-start.1 = ((bf16[8,96,3968]{2,1,0:T(8,128)(2,1)}), bf16[8,96,3968]{2,1,0:T(8,128)(2,1)}, u32[]{:S(2)}, u32[]{:S(2)}) async-start(bf16[8,96,3968]{2,1,0:T(8,128)(2,1)} %bitcast.80), calls=%async_computation.1 | async-start | bytes 12189696 | tf_op jit(solution)/shard_map/all_to_all | solution.py:197
  157.6 6.2 %copy-start.3 = (f32[128]{0:T(128)S(1)}, f32[128]{0:T(128)}, u32[]{:S(2)}) copy-start(f32[128]{0:T(128)} %param.9) | copy-start | bytes 1540
  157.6 142.2 %all-to-all-start.2 = ((bf16[8,96,4096]{2,1,0:T(8,128)(2,1)}), bf16[8,96,4096]{2,1,0:T(8,128)(2,1)}, u32[]{:S(2)}, u32[]{:S(2)}) async-start(bf16[8,96,4096]{2,1,0:T(8,128)(2,1)} %bitcast.79), calls=%async_computation.2 | async-start | bytes 12582912 | tf_op jit(solution)/shard_map/all_to_all | solution.py:197
  162.5 52.1 %all-gather.7.cloned.1.call-start = ((), (), s32[]{:S(2)}) async-start(), calls=%async_computation.3 | async-start | bytes 4587520 | tf_op jit(solution)/shard_map/all_gather | solution.py:246
  171.8 9.9 %copy-start = (f32[128]{0:T(128)S(1)}, f32[128]{0:T(128)}, u32[]{:S(2)}) copy-start(f32[128]{0:T(128)} %param.10) | copy-start | bytes 1540
  181.6 165.4 %all-gather.9.cloned.1.call-start = ((), (), s32[]{:S(2)}) async-start(), calls=%async_computation.4 | async-start | bytes 5242880 | tf_op jit(solution)/shard_map/all_gather | solution.py:246
Sparse Core Ops, SparseCore 0:
  181.7 32.7 all-gather.6
  310.9 34.7 all-gather.8

commit v5 on v4

--- a/solution.py
+++ b/solution.py
@@ -7,7 +7,7 @@
 
 TILE_HEADS = 8
 ROWS = 128
-GROUPS = (7, 8, 1)
+GROUPS = (6, 8, 2)
 LOG2E = 1.4426950408889634
 VMEM = 58 * 1024 * 1024
 

time: 375 us -> 367 us (0.979)
  waiting for transfers between devices: 215 us -> 200 us
  blocking collectives: 38.1 us -> 45.9 us
    all_to_all x1, blocking collectives: 23.8 us -> 40.7 us  [exchange(): lax.all_to_all(block, 'stream', split_axis=0, concat_axis=0, tiled=True)]
    all_to_all x2, waiting for transfers between devices: 196 us -> 184 us  [exchange(): lax.all_to_all(block, 'stream', split_axis=0, concat_axis=0, tiled=True)]
    all_gather x1 -> x0, blocking collectives: 9.33 us -> none  [on_device(): gathered = lax.all_gather(carried, 'pos')]
    all_gather x2 -> x3, waiting for transfers between devices: 18.8 us -> 15.7 us  [on_device(): gathered = lax.all_gather(carried, 'pos')]
  transfers between devices with their start and end apart: 4 -> 5, of which waited for: 3 -> 4; matrix products, arithmetic and copies ran while one was open for 7% -> 8% of each run, Pallas kernels for 7% -> 11%
where the time goes in v5:
time: 367 us; the launch traced here: 366 us
  waiting for transfers between devices  200 us (54%)
  Pallas kernels  57.9 us (16%)
  blocking collectives  45.9 us (13%)
  matrix products  18 us (5%)
  local copies, waits for them, and re-layouts  15.4 us (4%)
  between operations  13.3 us (4%)
  starting transfers between devices  12.2 us (3%)
  other arithmetic  3.83 us (1%)
    all_to_all x2, waiting for transfers between devices, exchange(): lax.all_to_all(block, 'stream', split_axis=0, concat_axis=0, tiled=True)  184 us
    all_to_all x1, blocking collectives, exchange(): lax.all_to_all(block, 'stream', split_axis=0, concat_axis=0, tiled=True)  40.7 us
    pallas_call x3, Pallas kernels, outputs(): pl.pallas_call(output_kernel, grid=(tiles,), in_specs=in_specs, out_specs...  34.2 us
    pallas_call x3, Pallas kernels, states(): pl.pallas_call(state_kernel, grid=(tiles,), in_specs=[pl.BlockSpec((rows,...  23.7 us
    all_gather x3, waiting for transfers between devices, on_device(): gathered = lax.all_gather(carried, 'pos')  15.7 us
    dot_general x3, matrix products, packed(): return jnp.dot(pack, block, preferred_element_type=jnp.bfloat16)  15.1 us
    all_to_all x2, starting transfers between devices, exchange(): lax.all_to_all(block, 'stream', split_axis=0, concat_axis=0, tiled=True)  12.1 us
    reshape x3, local copies, waits for them, and re-layouts, by_tile(): return jnp.moveaxis(array.reshape(rows, all_tiles, TILE_HEADS), 1, 0)  7.77 us
  transfers between devices with their start and end apart: 5, of which 4 were waited for; matrix products, arithmetic and copies ran while one was open for 8% of the time, Pallas kernels for 11%

profile of v5, /device:TPU:0, one launch (start us, length us, event | category | flops | bytes accessed | tf_op | source)
XLA Modules:
  0.0 366.4 jit_solution(15375269292284036200)
XLA Ops:
  6.5 0.7 fusion.25
  7.5 0.7 bitcast_subtract_fusion
  8.3 2.1 slice.42
  10.4 5.2 %fusion.2 = bf16[768,3456]{1,0:T(8,128)(2,1)} fusion(bf16[512,128]{1,0:T(8,128)(2,1)S(1)} %bitcast.99, bf16[512,256]{1,0:T(8,128)(2,1)S(1)} %bitcast.98, bf16[512,3072]{1,0:T(8,128)(2,1)S(1)} %slice.42, s32[768]{0:T(1024)S(1)} %add.60), kind=kOutput, calls=%fused_computation.2 | convolution fusion | flops 2728919040 | bytes 8850432 | tf_op jit(solution)/shard_map/dot_general | solution.py:192
  15.7 7.3 %all-to-all-start.1 = ((bf16[8,96,3456]{2,1,0:T(8,128)(2,1)}), bf16[8,96,3456]{2,1,0:T(8,128)(2,1)}, u32[]{:S(2)}, u32[]{:S(2)}) async-start(bf16[8,96,3456]{2,1,0:T(8,128)(2,1)} %bitcast.81), calls=%async_computation.1 | async-start | bytes 10616832 | tf_op jit(solution)/shard_map/all_to_all | solution.py:197
  22.9 2.2 fusion.8
  25.2 7.6 %fusion = bf16[768,4096]{1,0:T(8,128)(2,1)} fusion(bf16[512,8192]{1,0:T(8,128)(2,1)} %bitcast.89, s32[768]{0:T(1024)S(1)} %add.60), kind=kOutput, calls=%fused_computation | convolution fusion | flops 3221618688 | bytes 10488832 | tf_op jit(solution)/shard_map/dot_general | solution.py:192
  32.8 107.3 %all-to-all-done.1 = bf16[8,96,3456]{2,1,0:T(8,128)(2,1)} async-done(((bf16[8,96,3456]{2,1,0:T(8,128)(2,1)}), bf16[8,96,3456]{2,1,0:T(8,128)(2,1)}, u32[]{:S(2)}, u32[]{:S(2)}) %all-to-all-start.1) | async-done | bytes 5308448 | tf_op jit(solution)/shard_map/all_to_all | solution.py:197
  140.1 4.9 %all-to-all-start.2 = ((bf16[8,96,4096]{2,1,0:T(8,128)(2,1)}), bf16[8,96,4096]{2,1,0:T(8,128)(2,1)}, u32[]{:S(2)}, u32[]{:S(2)}) async-start(bf16[8,96,4096]{2,1,0:T(8,128)(2,1)} %bitcast.79), calls=%async_computation.2 | async-start | bytes 12582912 | tf_op jit(solution)/shard_map/all_to_all | solution.py:197
  145.0 0.9 dynamic-slice_reduce_fusion
  145.9 0.2 reduce-window.26
  146.2 1.1 fusion.10.order_ref
  147.4 1.6 fusion.9
  150.0 1.0 subtract_bitcast_fusion
  151.0 2.6 copy.26
  153.6 0.7 fusion.27
  154.2 8.7 %shard_map.65 = (bf16[512,3072]{1,0:T(8,128)(2,1)}, bf16[128,3072]{1,0:T(8,128)(2,1)}) custom-call(bf16[512,768]{1,0:T(8,128)(2,1)} %fusion.10.order_ref, bf16[768,3456]{1,0:T(8,128)(2,1)} %bitcast.10.arrived_ref, bf16[128,512]{1,0:T(8,128)(2,1)} %get-tuple-element.28.inputs_t_ref, f32[16,512,8]{2,1,0:T(8,128)} %bitcast.76), custom_call_target="tpu_custom_call" | custom-call | flops 2818572288 | bytes 8650752 | tf_op jit(solution)/shard_map/pallas_call | solution.py:95
  163.1 0.7 broadcast_in_dim_reshape.2.skip_ref
  163.8 0.8 copy.30.readout_ref
  164.6 2.6 copy.28
  167.2 2.6 copy.29
  169.8 5.2 %all-gather.3 = f32[4,1,128]{2,1,0:T(1,128)S(1)} all-gather(f32[1,1,128]{2,1,0:T(1,128)S(1)} %bitcast.96), channel_id=1, replica_groups=mesh['pos'=4,'stream'=8] {'pos'}, dimensions={0}, use_global_device_ids=true | all-gather | bytes 2560 | tf_op jit(solution)/shard_map/all_gather | solution.py:232
  175.3 0.8 reshape.205.coef_ref
  176.0 1.3 fusion.21.scores_ref
  177.3 15.6 %all-gather.10.cloned.1.call-done = bf16[512,3072]{1,0:T(8,128)(2,1)} async-done(((bf16[128,3072]{1,0:T(8,128)(2,1)}), bf16[512,3072]{1,0:T(8,128)(2,1)}) %all-gather.10.cloned.1.call-update) | async-done | bytes 3145744 | tf_op jit(solution)/shard_map/all_gather | solution.py:246
  192.9 12.4 %shard_map.66.rest_0_ = bf16[512,8192]{1,0:T(8,128)(2,1)} custom-call(bf16[512,3072]{1,0:T(8,128)(2,1)} %get-tuple-element.19.x_ref, f32[512,512]{1,0:T(8,128)} %fusion.21.scores_ref, bf16[512,128]{1,0:T(8,128)(2,1)} %copy.30.readout_ref, f32[16,512,8]{2,1,0:T(8,128)} %bitcast.70, f32[16,512,8]{2,1,0:T(8,128)} %bitcast.73, ...), custom_call_target="tpu_custom_call" | custom-call | flops 5234491392 | bytes 9437184 | tf_op jit(solution)/shard_map/pallas_call | solution.py:145
  205.4 76.9 %all-to-all-done.2 = bf16[8,96,4096]{2,1,0:T(8,128)(2,1)} async-done(((bf16[8,96,4096]{2,1,0:T(8,128)(2,1)}), bf16[8,96,4096]{2,1,0:T(8,128)(2,1)}, u32[]{:S(2)}, u32[]{:S(2)}) %all-to-all-start.2) | async-done | bytes 6291488 | tf_op jit(solution)/shard_map/all_to_all | solution.py:197
  282.3 10.9 %shard_map.67 = (bf16[512,4096]{1,0:T(8,128)(2,1)}, bf16[128,4096]{1,0:T(8,128)(2,1)}) custom-call(bf16[512,768]{1,0:T(8,128)(2,1)} %fusion.10.order_ref, bf16[768,4096]{1,0:T(8,128)(2,1)} %bitcast.26.arrived_ref, bf16[128,512]{1,0:T(8,128)(2,1)} %get-tuple-element.28.inputs_t_ref, f32[16,512,8]{2,1,0:T(8,128)} %bitcast.77), custom_call_target="tpu_custom_call" | custom-call | flops 3758096384 | bytes 11534336 | tf_op jit(solution)/shard_map/pallas_call | solution.py:95
  293.3 40.7 %all_to_all.15 = bf16[8,96,1024]{2,1,0:T(8,128)(2,1)} all-to-all(bf16[8,96,1024]{2,1,0:T(8,128)(2,1)S(1)} %bitcast.86), channel_id=1, replica_groups=mesh['pos'=4,'stream'=8] {'stream'}, dimensions={0} | all-to-all | bytes 3145728 | tf_op jit(solution)/shard_map/all_to_all | solution.py:197
  333.9 4.1 %shard_map.64 = (bf16[512,1024]{1,0:T(8,128)(2,1)}, bf16[128,1024]{1,0:T(8,128)(2,1)}) custom-call(bf16[512,768]{1,0:T(8,128)(2,1)} %fusion.10.order_ref, bf16[768,1024]{1,0:T(8,128)(2,1)} %bitcast.80, bf16[128,512]{1,0:T(8,128)(2,1)} %get-tuple-element.28.inputs_t_ref, f32[16,512,8]{2,1,0:T(8,128)} %bitcast.78), custom_call_target="tpu_custom_call" | custom-call | flops 939524096 | bytes 2883584 | tf_op jit(solution)/shard_map/pallas_call | solution.py:95
  338.1 15.8 %shard_map.68.rest_0_ = bf16[512,8192]{1,0:T(8,128)(2,1)} custom-call(bf16[512,4096]{1,0:T(8,128)(2,1)} %get-tuple-element.22.x_ref, f32[512,512]{1,0:T(8,128)} %fusion.21.scores_ref, bf16[512,128]{1,0:T(8,128)(2,1)} %copy.30.readout_ref, f32[16,512,8]{2,1,0:T(8,128)} %bitcast.71, f32[16,512,8]{2,1,0:T(8,128)} %bitcast.74, ...), custom_call_target="tpu_custom_call", output_to_operand_aliasing={{}: (9, {})} | custom-call | flops 6979321856 | bytes 12582912 | tf_op jit(solution)/shard_map/pallas_call | solution.py:145
  354.0 5.9 %shard_map.69 = bf16[512,8192]{1,0:T(8,128)(2,1)} custom-call(bf16[512,1024]{1,0:T(8,128)(2,1)} %get-tuple-element.16.x_ref, f32[512,512]{1,0:T(8,128)} %fusion.21.scores_ref, bf16[512,128]{1,0:T(8,128)(2,1)} %copy.30.readout_ref, f32[16,512,8]{2,1,0:T(8,128)} %bitcast.72, f32[16,512,8]{2,1,0:T(8,128)} %bitcast.75, ...), custom_call_target="tpu_custom_call", output_to_operand_aliasing={{}: (9, {})} | custom-call | flops 1744830464 | bytes 3145728 | tf_op jit(solution)/shard_map/pallas_call | solution.py:145
  (41 shorter events, 2.1 us)
Async XLA Ops:
  6.5 3.9 %copy-start.2 = (bf16[1,512,128]{2,1,0:T(8,128)(2,1)S(1)}, bf16[1,512,128]{2,1,0:T(8,128)(2,1)}, u32[]{:S(2)}) copy-start(bf16[1,512,128]{2,1,0:T(8,128)(2,1)} %param.8) | copy-start | bytes 393220
  6.5 3.9 %copy-start.1 = (bf16[1,512,256]{2,1,0:T(8,128)(2,1)S(1)}, bf16[1,512,256]{2,1,0:T(8,128)(2,1)}, u32[]{:S(2)}) copy-start(bf16[1,512,256]{2,1,0:T(8,128)(2,1)} %param.7) | copy-start | bytes 786436
  15.7 124.4 %all-to-all-start.1 = ((bf16[8,96,3456]{2,1,0:T(8,128)(2,1)}), bf16[8,96,3456]{2,1,0:T(8,128)(2,1)}, u32[]{:S(2)}, u32[]{:S(2)}) async-start(bf16[8,96,3456]{2,1,0:T(8,128)(2,1)} %bitcast.81), calls=%async_computation.1 | async-start | bytes 10616832 | tf_op jit(solution)/shard_map/all_to_all | solution.py:197
  140.1 6.2 %copy-start.3 = (f32[128]{0:T(128)S(1)}, f32[128]{0:T(128)}, u32[]{:S(2)}) copy-start(f32[128]{0:T(128)} %param.9) | copy-start | bytes 1540
  140.1 142.2 %all-to-all-start.2 = ((bf16[8,96,4096]{2,1,0:T(8,128)(2,1)}), bf16[8,96,4096]{2,1,0:T(8,128)(2,1)}, u32[]{:S(2)}, u32[]{:S(2)}) async-start(bf16[8,96,4096]{2,1,0:T(8,128)(2,1)} %bitcast.79), calls=%async_computation.2 | async-start | bytes 12582912 | tf_op jit(solution)/shard_map/all_to_all | solution.py:197
  145.0 48.0 %all-gather.10.cloned.1.call-start = ((), (), s32[]{:S(2)}) async-start(), calls=%async_computation.4 | async-start | bytes 3932160 | tf_op jit(solution)/shard_map/all_gather | solution.py:246
  154.2 8.8 %copy-start = (f32[128]{0:T(128)S(1)}, f32[128]{0:T(128)}, u32[]{:S(2)}) copy-start(f32[128]{0:T(128)} %param.10) | copy-start | bytes 1540
  163.0 175.1 %all-gather.12.cloned.1.call-start = ((), (), s32[]{:S(2)}) async-start(), calls=%async_computation.5 | async-start | bytes 5242880 | tf_op jit(solution)/shard_map/all_gather | solution.py:246
  293.2 60.8 %all-gather.8.cloned.1.call-start = ((), (), s32[]{:S(2)}) async-start(), calls=%async_computation.3 | async-start | bytes 1310720 | tf_op jit(solution)/shard_map/all_gather | solution.py:246
Sparse Core Ops, SparseCore 0:
  163.1 29.8 all-gather.9
  293.3 33.6 all-gather.11
  338.2 15.7 all-gather.7
